TPU v7x, 32 devices: a whole 2x2x4 slice. The times are simulated.
32 devices in a mesh: leaf: 32 (over z, y, x, core).
Axes of the slice: x: 2, y: 2, z: 4, core: 2. Of those that a mesh axis runs over, the one named last changes fastest.
Arguments:
- charges: bfloat16 [16, 262144], P(None, 'leaf'), may hold values from -6 to 6
- points: bfloat16 [3, 262144], P(None, 'leaf'), may hold values from 0 to 1
- leaf_basis: bfloat16 [256, 1024, 128], P('leaf'), may hold values from -0.1875 to 0.1875
- transfer: float32 [4, 2, 128, 128], replicated, may hold values from -0.375 to 0.375
- coupling: float32 [4, 3, 128, 128], replicated, may hold values from -0.5 to 0.5
- near_list: int32 [256, 5], P('leaf'), may hold values from 0 to 255, as said below
- couple_flags: int32 [32, 4, 3], P('leaf'), may hold values from 0 to 1, as said below
Outputs:
- potential: bfloat16 [16, 262144], P(None, 'leaf')
Inputs may be any that keep to these rules, and one draw needn't show every extreme that they name: `near_list`: entries of a row are distinct leaves within 32 of the row's leaf i; the first is i itself and the second lies exactly 32 away from i. `couple_flags`: at level t the flags are equal for all clusters c with equal c // 2^t.
All inputs are finite; a program needn't handle non-finite values.
Results may differ from a plain program's by a relative error of at most 0.0049.
Values may be sent and summed in bfloat16 or wider, within the bound.
A program may use at most 64 MiB of HBM per device.

v0:
```python
import math

import jax
import jax.numpy as jnp
from jax import lax
from jax.sharding import PartitionSpec as P

smoothing_sq = 0.01


def passed_along(block, axis, distance):
    devices = range(lax.axis_size(axis))
    route = [(i - distance, i) for i in devices if i - distance in devices]
    return lax.ppermute(block, axis, route)


def from_partner(array, axis, apart):
    return lax.ppermute(array, axis, [(i, i ^ 1 << apart) for i in range(lax.axis_size(axis))])


def positions(raw, leaf_num, leaf_step):
    coords = raw.astype(jnp.float32)
    return jnp.stack([coords[0] + leaf_num * leaf_step, coords[1], coords[2]], axis=0)


def kernel_block(src_pos, tgt_pos):
    diff_x = src_pos[0][:, None] - tgt_pos[0][None, :]
    diff_y = src_pos[1][:, None] - tgt_pos[1][None, :]
    diff_z = src_pos[2][:, None] - tgt_pos[2][None, :]
    dist_sq = diff_x * diff_x + diff_y * diff_y + diff_z * diff_z
    return lax.rsqrt(dist_sq + smoothing_sq).astype(jnp.bfloat16)


def local(charges, points, leaf_basis, transfer, coupling, near_list, couple_flags):
    highest = lax.Precision.HIGHEST
    device_id = lax.axis_index("leaf")
    leaves_dev = leaf_basis.shape[0]
    leaf_rows = leaf_basis.shape[1]
    rhs_count = charges.shape[0]
    cluster_rows = leaves_dev * leaf_rows
    levels = transfer.shape[0]
    neighbours = near_list.shape[1]
    reach = 4
    leaf_step = 1.0 / (2.0 * reach * leaves_dev)
    pieces = {0: (charges, points)}
    for offset in range(-reach, reach + 1):
        if offset != 0:
            pieces[offset] = passed_along((charges, points), "leaf", -offset)
    window_vals = jnp.concatenate([pieces[o][0] for o in range(-reach, reach + 1)], axis=1)
    window_pos = jnp.concatenate([pieces[o][1] for o in range(-reach, reach + 1)], axis=1)
    base_leaf = (device_id - reach) * leaves_dev

    def near_leaf(a, accumulated):
        global_leaf = device_id * leaves_dev + a
        tgt_pos = positions(
            lax.dynamic_slice(points, (jnp.int32(0), a * leaf_rows), (3, leaf_rows)),
            global_leaf.astype(jnp.float32),
            leaf_step,
        )
        row_list = lax.dynamic_index_in_dim(near_list, a, 0, keepdims=False)
        near_sum = jnp.zeros((rhs_count, leaf_rows), jnp.float32)
        for k in range(neighbours):
            j = row_list[k]
            start = (j - base_leaf) * leaf_rows
            src_pos = positions(
                lax.dynamic_slice(window_pos, (jnp.int32(0), start), (3, leaf_rows)),
                j.astype(jnp.float32),
                leaf_step,
            )
            src_vals = lax.dynamic_slice(window_vals, (jnp.int32(0), start), (rhs_count, leaf_rows))
            near_sum = near_sum + jnp.dot(
                src_vals, kernel_block(src_pos, tgt_pos), preferred_element_type=jnp.float32
            )
        return lax.dynamic_update_slice(accumulated, near_sum, (jnp.int32(0), a * leaf_rows))

    near_field = lax.fori_loop(
        0, leaves_dev, near_leaf, jnp.zeros((rhs_count, cluster_rows), jnp.float32)
    )
    basis_rows = leaf_basis.reshape(cluster_rows, leaf_basis.shape[2])
    first_coef = jnp.dot(charges, basis_rows, preferred_element_type=jnp.float32)
    flag_vals = couple_flags[0].astype(jnp.float32)
    coupled_levels = []
    own_coef = first_coef
    sib_coef = from_partner(first_coef, "leaf", 0)
    for t in range(levels):
        child_side = device_id // 2**t % 2
        cousin_even, cousin_odd = from_partner((own_coef, sib_coef), "leaf", t + 1)
        partners = (sib_coef, cousin_even, cousin_odd)
        coupled = jnp.zeros(first_coef.shape, jnp.float32)
        for m in range(3):
            product = jnp.dot(
                partners[m], coupling[t, m], precision=highest, preferred_element_type=jnp.float32
            )
            coupled = coupled + flag_vals[t, m] * product
        coupled_levels.append(coupled)
        if t + 1 < levels:

            def merge_children(first_child, second_child):
                left_coef = jnp.where(child_side == 0, first_child, second_child)
                right_coef = jnp.where(child_side == 0, second_child, first_child)
                return jnp.dot(
                    left_coef, transfer[t, 0], precision=highest, preferred_element_type=jnp.float32
                ) + jnp.dot(
                    right_coef,
                    transfer[t, 1],
                    precision=highest,
                    preferred_element_type=jnp.float32,
                )

            own_coef, sib_coef = (
                merge_children(own_coef, sib_coef),
                merge_children(cousin_even, cousin_odd),
            )
    local_coef = coupled_levels[-1]
    for t in range(levels - 1, 0, -1):
        child_side = device_id // 2 ** (t - 1) % 2
        transfer_mat = lax.dynamic_index_in_dim(transfer[t - 1], child_side, 0, keepdims=False)
        local_coef = coupled_levels[t - 1] + lax.dot_general(
            local_coef,
            transfer_mat,
            (((1,), (1,)), ((), ())),
            precision=highest,
            preferred_element_type=jnp.float32,
        )
    local_bf = local_coef.astype(jnp.bfloat16)
    far_field = lax.dot_general(
        local_bf, basis_rows, (((1,), (1,)), ((), ())), preferred_element_type=jnp.float32
    )
    near_scale = 1.0 / math.sqrt(neighbours * leaf_rows)
    return (near_field * near_scale + far_field).astype(jnp.bfloat16)


def solution(mesh):
    return jax.shard_map(
        local,
        mesh=mesh,
        in_specs=(
            P(None, "leaf"),
            P(None, "leaf"),
            P("leaf", None, None),
            P(),
            P(),
            P("leaf", None),
            P("leaf", None, None),
        ),
        out_specs=P(None, "leaf"),
        check_vma=False,
    )
```

profile of v0, /device:TPU:12, one launch (start us, length us, event | category | flops | bytes accessed | tf_op | source)
XLA Modules:
  0.0 305.7 jit_solution(14251049574841617838)
XLA Ops:
  4.6 3.4 %collective-permute-start = (bf16[16,8192]{1,0:T(8,128)(2,1)S(1)}, bf16[16,8192]{1,0:T(8,128)(2,1)}, u32[]{:S(2)}, u32[]{:S(2)}) collective-permute-start(bf16[16,8192]{1,0:T(8,128)(2,1)S(1)} %copy-done.2), channel_id=1, source_target_pairs={{0,4},{1,5},{2,6},{3,7},{4,8},{5,9},{6,10},{7,11},{8,12},{9,13},{1... | collective-permute-start | bytes 786440 | tf_op jit(solution)/shard_map/ppermute | solution.py:14
  8.0 1.9 collective-permute-start.1
  9.9 4.4 %collective-permute-start.2 = (bf16[16,8192]{1,0:T(8,128)(2,1)S(1)}, bf16[16,8192]{1,0:T(8,128)(2,1)S(1)}, u32[]{:S(2)}, u32[]{:S(2)}) collective-permute-start(bf16[16,8192]{1,0:T(8,128)(2,1)S(1)} %copy-done.2), channel_id=1, source_target_pairs={{0,2},{1,3},{2,4},{3,5},{4,6},{5,7},{6,8},{7,9},{8,10},{9,11},{10,... | collective-permute-start | bytes 786440 | tf_op jit(solution)/shard_map/ppermute | solution.py:14
  16.9 1.9 collective-permute-start.3
  19.9 1.9 collective-permute-start.18
  25.0 3.9 %collective-permute-done.18 = f32[16,128]{1,0:T(8,128)S(1)} collective-permute-done((f32[16,128]{1,0:T(8,128)}, f32[16,128]{1,0:T(8,128)S(1)}, u32[]{:S(2)}, u32[]{:S(2)}) %collective-permute-start.18) | collective-permute-done | bytes 8224 | tf_op jit(solution)/shard_map/ppermute | solution.py:18
  52.7 3.7 %collective-permute-start.8 = (bf16[3,8192]{1,0:T(4,128)(2,1)}, bf16[3,8192]{1,0:T(4,128)(2,1)S(1)}, u32[]{:S(2)}, u32[]{:S(2)}) collective-permute-start(bf16[3,8192]{1,0:T(4,128)(2,1)} %param.10), channel_id=1, source_target_pairs={{0,4},{1,5},{2,6},{3,7},{4,8},{5,9},{6,10},{7,11},{8,12},{9,13},{1... | collective-permute-start | bytes 147464 | tf_op jit(solution)/shard_map/ppermute | solution.py:14
  64.4 1.9 collective-permute-start.9
  66.9 3.0 collective-permute-done.9
  70.0 1.9 collective-permute-start.10
  72.5 4.5 %collective-permute-done.10 = bf16[3,8192]{1,0:T(4,128)(2,1)S(1)} collective-permute-done((bf16[3,8192]{1,0:T(4,128)(2,1)S(1)}, bf16[3,8192]{1,0:T(4,128)(2,1)S(1)}, u32[]{:S(2)}, u32[]{:S(2)}) %collective-permute-start.10) | collective-permute-done | bytes 49184 | tf_op jit(solution)/shard_map/ppermute | solution.py:14
  79.6 3.9 %collective-permute-done.11 = bf16[3,8192]{1,0:T(4,128)(2,1)S(1)} collective-permute-done((bf16[3,8192]{1,0:T(4,128)(2,1)S(1)}, bf16[3,8192]{1,0:T(4,128)(2,1)S(1)}, u32[]{:S(2)}, u32[]{:S(2)}) %collective-permute-start.11) | collective-permute-done | bytes 49184 | tf_op jit(solution)/shard_map/ppermute | solution.py:14
  89.8 3.6 %collective-permute-done.13 = bf16[3,8192]{1,0:T(4,128)(2,1)S(1)} collective-permute-done((bf16[3,8192]{1,0:T(4,128)(2,1)S(1)}, bf16[3,8192]{1,0:T(4,128)(2,1)S(1)}, u32[]{:S(2)}, u32[]{:S(2)}) %collective-permute-start.13) | collective-permute-done | bytes 49184 | tf_op jit(solution)/shard_map/ppermute | solution.py:14
  93.4 5.2 %collective-permute-start.14 = (bf16[3,8192]{1,0:T(4,128)(2,1)S(1)}, bf16[3,8192]{1,0:T(4,128)(2,1)S(1)}, u32[]{:S(2)}, u32[]{:S(2)}) collective-permute-start(bf16[3,8192]{1,0:T(4,128)(2,1)S(1)} %copy-done.3), channel_id=1, source_target_pairs={{3,0},{4,1},{5,2},{6,3},{7,4},{8,5},{9,6},{10,7},{11,8},{12,9},{13... | collective-permute-start | bytes 147464 | tf_op jit(solution)/shard_map/ppermute | solution.py:14
  99.2 3.9 %collective-permute-done.14 = bf16[3,8192]{1,0:T(4,128)(2,1)S(1)} collective-permute-done((bf16[3,8192]{1,0:T(4,128)(2,1)S(1)}, bf16[3,8192]{1,0:T(4,128)(2,1)S(1)}, u32[]{:S(2)}, u32[]{:S(2)}) %collective-permute-start.14) | collective-permute-done | bytes 49184 | tf_op jit(solution)/shard_map/ppermute | solution.py:14
  103.1 1.9 collective-permute-start.15
  105.7 4.5 %collective-permute-done.15 = bf16[3,8192]{1,0:T(4,128)(2,1)S(1)} collective-permute-done((bf16[3,8192]{1,0:T(4,128)(2,1)S(1)}, bf16[3,8192]{1,0:T(4,128)(2,1)S(1)}, u32[]{:S(2)}, u32[]{:S(2)}) %collective-permute-start.15) | collective-permute-done | bytes 49184 | tf_op jit(solution)/shard_map/ppermute | solution.py:14
  110.2 2.4 collective-permute-start.4
  113.2 2.0 collective-permute-start.5
  116.2 4.6 %collective-permute-start.6 = (bf16[16,8192]{1,0:T(8,128)(2,1)S(1)}, bf16[16,8192]{1,0:T(8,128)(2,1)S(1)}, u32[]{:S(2)}, u32[]{:S(2)}) collective-permute-start(bf16[16,8192]{1,0:T(8,128)(2,1)S(1)} %copy-done.2), channel_id=1, source_target_pairs={{3,0},{4,1},{5,2},{6,3},{7,4},{8,5},{9,6},{10,7},{11,8},{12,9},{13... | collective-permute-start | bytes 786440 | tf_op jit(solution)/shard_map/ppermute | solution.py:14
  121.8 2.3 collective-permute-start.7
  124.6 2.4 collective-permute-done.6
  127.1 11.2 %collective-permute-done.7 = bf16[16,8192]{1,0:T(8,128)(2,1)S(1)} collective-permute-done((bf16[16,8192]{1,0:T(8,128)(2,1)S(1)}, bf16[16,8192]{1,0:T(8,128)(2,1)S(1)}, u32[]{:S(2)}, u32[]{:S(2)}) %collective-permute-start.7) | collective-permute-done | bytes 262176 | tf_op jit(solution)/shard_map/ppermute | solution.py:14
  139.8 165.2 %while.15 = (s32[]{:T(128)}, f32[16,8192]{1,0:T(8,128)S(1)}, s32[8,5]{1,0:T(8,128)}, s32[]{:T(128)}, bf16[16,73728]{1,0:T(8,128)(2,1)}, /*index=5*/bf16[3,73728]...) while((s32[]{:T(128)}, f32[16,8192]{1,0:T(8,128)S(1)}, ...), condition=%wide.region_1.2_spmd, body=%wide.region_0.1_spmd.sunk | while | flops 220291104 | bytes 1135349 | solution.py:76
  145.7 2.4 fusion.168
  148.8 2.4 fusion.169
  151.9 2.4 fusion.170
  155.0 2.4 fusion.171
  158.0 2.4 fusion.172
  166.4 2.4 fusion.168
  169.4 2.4 fusion.169
  172.5 2.4 fusion.170
  175.6 2.4 fusion.171
  178.6 2.4 fusion.172
  187.1 2.4 fusion.168
  190.1 2.4 fusion.169
  193.2 2.4 fusion.170
  196.3 2.4 fusion.171
  199.3 2.4 fusion.172
  207.7 2.4 fusion.168
  210.8 2.4 fusion.169
  213.8 2.4 fusion.170
  217.0 2.4 fusion.171
  219.9 2.4 fusion.172
  228.4 2.4 fusion.168
  231.4 2.4 fusion.169
  234.5 2.4 fusion.170
  237.6 2.4 fusion.171
  240.6 2.4 fusion.172
  249.0 2.4 fusion.168
  252.1 2.4 fusion.169
  255.1 2.4 fusion.170
  258.3 2.4 fusion.171
  261.2 2.4 fusion.172
  269.7 2.4 fusion.168
  272.7 2.4 fusion.169
  275.8 2.4 fusion.170
  278.9 2.4 fusion.171
  281.9 2.4 fusion.172
  290.3 2.4 fusion.168
  293.4 2.4 fusion.169
  296.4 2.4 fusion.170
  299.6 2.4 fusion.171
  302.6 2.4 fusion.172
  (164 shorter events, 77.6 us)
Async XLA Ops:
  0.0 1.6 copy-start
  0.0 4.6 %copy-start.2 = (bf16[16,8192]{1,0:T(8,128)(2,1)S(1)}, bf16[16,8192]{1,0:T(8,128)(2,1)}, u32[]{:S(2)}) copy-start(bf16[16,8192]{1,0:T(8,128)(2,1)} %param.9) | copy-start | bytes 786436
  0.0 14.3 %copy-start.5 = (s32[1,4,3]{1,0,2:T(1,128)S(1)}, s32[1,4,3]{1,0,2:T(1,128)}, u32[]{:S(2)}) copy-start(s32[1,4,3]{1,0,2:T(1,128)} %param.15) | copy-start | bytes 148
  0.0 15.0 %copy-start.1 = (f32[4,2,128,128]{3,2,1,0:T(8,128)S(1)}, f32[4,2,128,128]{3,2,1,0:T(8,128)}, u32[]{:S(2)}) copy-start(f32[4,2,128,128]{3,2,1,0:T(8,128)} %param.12) | copy-start | bytes 1572868
  2.9 14.0 %collective-permute-start.16 = (f32[16,128]{1,0:T(8,128)S(1)}, f32[16,128]{1,0:T(8,128)}, u32[]{:S(2)}, u32[]{:S(2)}) collective-permute-start(f32[16,128]{1,0:T(8,128)S(1)} %fusion.130), channel_id=1, source_target_pairs={{0,1},{1,0},{2,3},{3,2},{4,5},{5,4},{6,7},{7,6},{8,9},{9,8},{10,11... | collective-permute-start | bytes 24584 | tf_op jit(solution)/shard_map/ppermute | solution.py:18
  3.0 16.9 %collective-permute-start.17 = (f32[16,128]{1,0:T(8,128)S(1)}, f32[16,128]{1,0:T(8,128)S(1)}, u32[]{:S(2)}, u32[]{:S(2)}) collective-permute-start(f32[16,128]{1,0:T(8,128)S(1)} %fusion.130), channel_id=1, source_target_pairs={{0,2},{1,3},{2,0},{3,1},{4,6},{5,7},{6,4},{7,5},{8,10},{9,11},{10,... | collective-permute-start | bytes 24584 | tf_op jit(solution)/shard_map/ppermute | solution.py:18
  4.6 108.6 %collective-permute-start = (bf16[16,8192]{1,0:T(8,128)(2,1)S(1)}, bf16[16,8192]{1,0:T(8,128)(2,1)}, u32[]{:S(2)}, u32[]{:S(2)}) collective-permute-start(bf16[16,8192]{1,0:T(8,128)(2,1)S(1)} %copy-done.2), channel_id=1, source_target_pairs={{0,4},{1,5},{2,6},{3,7},{4,8},{5,9},{6,10},{7,11},{8,12},{9,13},{1... | collective-permute-start | bytes 786440 | tf_op jit(solution)/shard_map/ppermute | solution.py:14
  8.0 108.2 %collective-permute-start.1 = (bf16[16,8192]{1,0:T(8,128)(2,1)S(1)}, bf16[16,8192]{1,0:T(8,128)(2,1)}, u32[]{:S(2)}, u32[]{:S(2)}) collective-permute-start(bf16[16,8192]{1,0:T(8,128)(2,1)S(1)} %copy-done.2), channel_id=1, source_target_pairs={{0,3},{1,4},{2,5},{3,6},{4,7},{5,8},{6,9},{7,10},{8,11},{9,12},{10... | collective-permute-start | bytes 786440 | tf_op jit(solution)/shard_map/ppermute | solution.py:14
  9.9 111.9 %collective-permute-start.2 = (bf16[16,8192]{1,0:T(8,128)(2,1)S(1)}, bf16[16,8192]{1,0:T(8,128)(2,1)S(1)}, u32[]{:S(2)}, u32[]{:S(2)}) collective-permute-start(bf16[16,8192]{1,0:T(8,128)(2,1)S(1)} %copy-done.2), channel_id=1, source_target_pairs={{0,2},{1,3},{2,4},{3,5},{4,6},{5,7},{6,8},{7,9},{8,10},{9,11},{10,... | collective-permute-start | bytes 786440 | tf_op jit(solution)/shard_map/ppermute | solution.py:14
  16.9 107.2 %collective-permute-start.3 = (bf16[16,8192]{1,0:T(8,128)(2,1)S(1)}, bf16[16,8192]{1,0:T(8,128)(2,1)S(1)}, u32[]{:S(2)}, u32[]{:S(2)}) collective-permute-start(bf16[16,8192]{1,0:T(8,128)(2,1)S(1)} %copy-done.2), channel_id=1, source_target_pairs={{0,1},{1,2},{2,3},{3,4},{4,5},{5,6},{6,7},{7,8},{8,9},{9,10},{10,1... | collective-permute-start | bytes 786440 | tf_op jit(solution)/shard_map/ppermute | solution.py:14
  19.9 9.0 %collective-permute-start.18 = (f32[16,128]{1,0:T(8,128)}, f32[16,128]{1,0:T(8,128)S(1)}, u32[]{:S(2)}, u32[]{:S(2)}) collective-permute-start(f32[16,128]{1,0:T(8,128)} %collective-permute-done.16), channel_id=1, source_target_pairs={{0,2},{1,3},{2,0},{3,1},{4,6},{5,7},{6,4},{7,5},{8,10},{9,11},{10,... | collective-permute-start | bytes 24584 | tf_op jit(solution)/shard_map/ppermute | solution.py:18
  28.9 3.7 %collective-permute-start.19 = (f32[16,128]{1,0:T(8,128)S(1)}, f32[16,128]{1,0:T(8,128)S(1)}, u32[]{:S(2)}, u32[]{:S(2)}) collective-permute-start(f32[16,128]{1,0:T(8,128)S(1)} %convolution_add_fusion.4), channel_id=1, source_target_pairs={{0,4},{1,5},{2,6},{3,7},{4,0},{5,1},{6,2},{7,3},{8,12},{9,13},{10,... | collective-permute-start | bytes 24584 | tf_op jit(solution)/shard_map/ppermute | solution.py:18
  29.1 35.3 %copy-start.3 = (bf16[3,8192]{1,0:T(4,128)(2,1)S(1)}, bf16[3,8192]{1,0:T(4,128)(2,1)}, u32[]{:S(2)}) copy-start(bf16[3,8192]{1,0:T(4,128)(2,1)} %param.10) | copy-start | bytes 147460
  32.6 3.7 %collective-permute-start.20 = (f32[16,128]{1,0:T(8,128)S(1)}, f32[16,128]{1,0:T(8,128)S(1)}, u32[]{:S(2)}, u32[]{:S(2)}) collective-permute-start(f32[16,128]{1,0:T(8,128)S(1)} %convolution_add_fusion.5), channel_id=1, source_target_pairs={{0,4},{1,5},{2,6},{3,7},{4,0},{5,1},{6,2},{7,3},{8,12},{9,13},{10,... | collective-permute-start | bytes 24584 | tf_op jit(solution)/shard_map/ppermute | solution.py:18
  36.2 3.7 %collective-permute-start.21 = (f32[16,128]{1,0:T(8,128)S(1)}, f32[16,128]{1,0:T(8,128)S(1)}, u32[]{:S(2)}, u32[]{:S(2)}) collective-permute-start(f32[16,128]{1,0:T(8,128)S(1)} %convolution_add_fusion.2), channel_id=1, source_target_pairs={{0,8},{1,9},{2,10},{3,11},{4,12},{5,13},{6,14},{7,15},{8,0},{9,1},... | collective-permute-start | bytes 24584 | tf_op jit(solution)/shard_map/ppermute | solution.py:18
  39.9 3.7 %collective-permute-start.22 = (f32[16,128]{1,0:T(8,128)S(1)}, f32[16,128]{1,0:T(8,128)S(1)}, u32[]{:S(2)}, u32[]{:S(2)}) collective-permute-start(f32[16,128]{1,0:T(8,128)S(1)} %convolution_add_fusion.3), channel_id=1, source_target_pairs={{0,8},{1,9},{2,10},{3,11},{4,12},{5,13},{6,14},{7,15},{8,0},{9,1},... | collective-permute-start | bytes 24584 | tf_op jit(solution)/shard_map/ppermute | solution.py:18
  43.6 4.5 %collective-permute-start.23 = (f32[16,128]{1,0:T(8,128)S(1)}, f32[16,128]{1,0:T(8,128)S(1)}, u32[]{:S(2)}, u32[]{:S(2)}) collective-permute-start(f32[16,128]{1,0:T(8,128)S(1)} %convolution_add_fusion), channel_id=1, source_target_pairs={{0,16},{1,17},{2,18},{3,19},{4,20},{5,21},{6,22},{7,23},{8,24},{9,... | collective-permute-start | bytes 24584 | tf_op jit(solution)/shard_map/ppermute | solution.py:18
  48.1 4.5 %collective-permute-start.24 = (f32[16,128]{1,0:T(8,128)S(1)}, f32[16,128]{1,0:T(8,128)S(1)}, u32[]{:S(2)}, u32[]{:S(2)}) collective-permute-start(f32[16,128]{1,0:T(8,128)S(1)} %convolution_add_fusion.1), channel_id=1, source_target_pairs={{0,16},{1,17},{2,18},{3,19},{4,20},{5,21},{6,22},{7,23},{8,24},{9,... | collective-permute-start | bytes 24584 | tf_op jit(solution)/shard_map/ppermute | solution.py:18
  52.7 11.7 %collective-permute-start.8 = (bf16[3,8192]{1,0:T(4,128)(2,1)}, bf16[3,8192]{1,0:T(4,128)(2,1)S(1)}, u32[]{:S(2)}, u32[]{:S(2)}) collective-permute-start(bf16[3,8192]{1,0:T(4,128)(2,1)} %param.10), channel_id=1, source_target_pairs={{0,4},{1,5},{2,6},{3,7},{4,8},{5,9},{6,10},{7,11},{8,12},{9,13},{1... | collective-permute-start | bytes 147464 | tf_op jit(solution)/shard_map/ppermute | solution.py:14
  64.4 5.6 %collective-permute-start.9 = (bf16[3,8192]{1,0:T(4,128)(2,1)S(1)}, bf16[3,8192]{1,0:T(4,128)(2,1)S(1)}, u32[]{:S(2)}, u32[]{:S(2)}) collective-permute-start(bf16[3,8192]{1,0:T(4,128)(2,1)S(1)} %copy-done.3), channel_id=1, source_target_pairs={{0,3},{1,4},{2,5},{3,6},{4,7},{5,8},{6,9},{7,10},{8,11},{9,12},{10... | collective-permute-start | bytes 147464 | tf_op jit(solution)/shard_map/ppermute | solution.py:14
  70.0 7.0 %collective-permute-start.10 = (bf16[3,8192]{1,0:T(4,128)(2,1)S(1)}, bf16[3,8192]{1,0:T(4,128)(2,1)S(1)}, u32[]{:S(2)}, u32[]{:S(2)}) collective-permute-start(bf16[3,8192]{1,0:T(4,128)(2,1)S(1)} %copy-done.3), channel_id=1, source_target_pairs={{0,2},{1,3},{2,4},{3,5},{4,6},{5,7},{6,8},{7,9},{8,10},{9,11},{10,... | collective-permute-start | bytes 147464 | tf_op jit(solution)/shard_map/ppermute | solution.py:14
  77.0 6.5 %collective-permute-start.11 = (bf16[3,8192]{1,0:T(4,128)(2,1)S(1)}, bf16[3,8192]{1,0:T(4,128)(2,1)S(1)}, u32[]{:S(2)}, u32[]{:S(2)}) collective-permute-start(bf16[3,8192]{1,0:T(4,128)(2,1)S(1)} %copy-done.3), channel_id=1, source_target_pairs={{0,1},{1,2},{2,3},{3,4},{4,5},{5,6},{6,7},{7,8},{8,9},{9,10},{10,1... | collective-permute-start | bytes 147464 | tf_op jit(solution)/shard_map/ppermute | solution.py:14
  83.5 3.8 %collective-permute-start.12 = (bf16[3,8192]{1,0:T(4,128)(2,1)S(1)}, bf16[3,8192]{1,0:T(4,128)(2,1)S(1)}, u32[]{:S(2)}, u32[]{:S(2)}) collective-permute-start(bf16[3,8192]{1,0:T(4,128)(2,1)S(1)} %copy-done.3), channel_id=1, source_target_pairs={{1,0},{2,1},{3,2},{4,3},{5,4},{6,5},{7,6},{8,7},{9,8},{10,9},{11,1... | collective-permute-start | bytes 147464 | tf_op jit(solution)/shard_map/ppermute | solution.py:14
  87.3 6.1 %collective-permute-start.13 = (bf16[3,8192]{1,0:T(4,128)(2,1)S(1)}, bf16[3,8192]{1,0:T(4,128)(2,1)S(1)}, u32[]{:S(2)}, u32[]{:S(2)}) collective-permute-start(bf16[3,8192]{1,0:T(4,128)(2,1)S(1)} %copy-done.3), channel_id=1, source_target_pairs={{2,0},{3,1},{4,2},{5,3},{6,4},{7,5},{8,6},{9,7},{10,8},{11,9},{12,... | collective-permute-start | bytes 147464 | tf_op jit(solution)/shard_map/ppermute | solution.py:14
  93.4 9.7 %collective-permute-start.14 = (bf16[3,8192]{1,0:T(4,128)(2,1)S(1)}, bf16[3,8192]{1,0:T(4,128)(2,1)S(1)}, u32[]{:S(2)}, u32[]{:S(2)}) collective-permute-start(bf16[3,8192]{1,0:T(4,128)(2,1)S(1)} %copy-done.3), channel_id=1, source_target_pairs={{3,0},{4,1},{5,2},{6,3},{7,4},{8,5},{9,6},{10,7},{11,8},{12,9},{13... | collective-permute-start | bytes 147464 | tf_op jit(solution)/shard_map/ppermute | solution.py:14
  103.1 7.0 %collective-permute-start.15 = (bf16[3,8192]{1,0:T(4,128)(2,1)S(1)}, bf16[3,8192]{1,0:T(4,128)(2,1)S(1)}, u32[]{:S(2)}, u32[]{:S(2)}) collective-permute-start(bf16[3,8192]{1,0:T(4,128)(2,1)S(1)} %copy-done.3), channel_id=1, source_target_pairs={{4,0},{5,1},{6,2},{7,3},{8,4},{9,5},{10,6},{11,7},{12,8},{13,9},{1... | collective-permute-start | bytes 147464 | tf_op jit(solution)/shard_map/ppermute | solution.py:14
  110.2 14.0 %collective-permute-start.4 = (bf16[16,8192]{1,0:T(8,128)(2,1)S(1)}, bf16[16,8192]{1,0:T(8,128)(2,1)S(1)}, u32[]{:S(2)}, u32[]{:S(2)}) collective-permute-start(bf16[16,8192]{1,0:T(8,128)(2,1)S(1)} %copy-done.2), channel_id=1, source_target_pairs={{1,0},{2,1},{3,2},{4,3},{5,4},{6,5},{7,6},{8,7},{9,8},{10,9},{11,1... | collective-permute-start | bytes 786440 | tf_op jit(solution)/shard_map/ppermute | solution.py:14
  113.2 11.4 %collective-permute-start.5 = (bf16[16,8192]{1,0:T(8,128)(2,1)S(1)}, bf16[16,8192]{1,0:T(8,128)(2,1)S(1)}, u32[]{:S(2)}, u32[]{:S(2)}) collective-permute-start(bf16[16,8192]{1,0:T(8,128)(2,1)S(1)} %copy-done.2), channel_id=1, source_target_pairs={{2,0},{3,1},{4,2},{5,3},{6,4},{7,5},{8,6},{9,7},{10,8},{11,9},{12,... | collective-permute-start | bytes 786440 | tf_op jit(solution)/shard_map/ppermute | solution.py:14
  116.2 10.9 %collective-permute-start.6 = (bf16[16,8192]{1,0:T(8,128)(2,1)S(1)}, bf16[16,8192]{1,0:T(8,128)(2,1)S(1)}, u32[]{:S(2)}, u32[]{:S(2)}) collective-permute-start(bf16[16,8192]{1,0:T(8,128)(2,1)S(1)} %copy-done.2), channel_id=1, source_target_pairs={{3,0},{4,1},{5,2},{6,3},{7,4},{8,5},{9,6},{10,7},{11,8},{12,9},{13... | collective-permute-start | bytes 786440 | tf_op jit(solution)/shard_map/ppermute | solution.py:14
  121.8 16.5 %collective-permute-start.7 = (bf16[16,8192]{1,0:T(8,128)(2,1)S(1)}, bf16[16,8192]{1,0:T(8,128)(2,1)S(1)}, u32[]{:S(2)}, u32[]{:S(2)}) collective-permute-start(bf16[16,8192]{1,0:T(8,128)(2,1)S(1)} %copy-done.2), channel_id=1, source_target_pairs={{4,0},{5,1},{6,2},{7,3},{8,4},{9,5},{10,6},{11,7},{12,8},{13,9},{1... | collective-permute-start | bytes 786440 | tf_op jit(solution)/shard_map/ppermute | solution.py:14
  138.3 1.4 copy-start.4
where the time goes:
time: 311 us; the launch traced here: 306 us
  matrix products  121 us (39%)
  starting transfers between devices  52 us (17%)
  loops' own time  51.2 us (16%)
  waiting for transfers between devices  49.1 us (16%)
  local copies, waits for them, and re-layouts  24.3 us (8%)
  other arithmetic  7.74 us (2%)
    dot_general x40, matrix products, near_leaf(): jnp.dot(src_vals, kernel_block(src_pos, tgt_pos), preferred_element_type=...  96.2 us
    another operation x1, loops' own time, local(): lax.fori_loop(0, leaves_dev, near_leaf, jnp.zeros((rhs_count, cluster_row...  51.2 us
    ppermute x16, starting transfers between devices, passed_along(): return lax.ppermute(block, axis, route)  43.3 us
    ppermute x16, waiting for transfers between devices, passed_along(): return lax.ppermute(block, axis, route)  38 us
    dot_general x12, matrix products, local(): jnp.dot(partners[m], coupling[t, m], precision=highest, preferred_element...  19.7 us
    ppermute x9, waiting for transfers between devices, from_partner(): lax.ppermute(array, axis, [(i, i ^ 1 << apart) for i in range(lax.axis_si...  11.1 us
    unnamed x28, local copies, waits for them, and re-layouts  10.2 us
    ppermute x9, starting transfers between devices, from_partner(): lax.ppermute(array, axis, [(i, i ^ 1 << apart) for i in range(lax.axis_si...  8.7 us
  transfers between devices with their start and end apart: 25, of which 17 were waited for; matrix products, arithmetic and copies ran while one was open for 11% of the time, Pallas kernels for 0%

commit v1 on v0

v1 whole, which is shorter than its diff:
```python
import functools
import math

import jax
import jax.numpy as jnp
from jax import lax
from jax.experimental import pallas as pl
from jax.experimental.pallas import tpu as pltpu
from jax.sharding import PartitionSpec as P

smoothing_sq = 0.01
reach = 4
tile = 256
f32 = jnp.float32
bf16 = jnp.bfloat16
MESH = pl.DeviceIdType.MESH


def split3(v):
    hi = v.astype(bf16).astype(f32)
    rest = v - hi
    mid = rest.astype(bf16).astype(f32)
    return hi, mid, rest - mid


def near_kernel(n, leaves, neighbours, near_ref, charges_ref, points_ref, out_ref, win, pos, send_sem, recv_sem):
    me = lax.axis_index("leaf")
    core = me % 2
    sibling = me + 1 - 2 * core
    rows = out_ref.shape[-1]
    leaf_step = 1.0 / (2.0 * reach * leaves)

    def each(off, body):
        @pl.when((me + off >= 0) & (me + off < n))
        def _():
            body()

    barrier = pltpu.get_barrier_semaphore()
    pl.semaphore_signal(barrier, inc=1, device_id=(sibling,), device_id_type=MESH)
    for off in (-4, -2, 2, 4):
        each(off, lambda: pl.semaphore_signal(barrier, inc=1, device_id=(me + off,), device_id_type=MESH))

    for l in range(leaves):
        win[reach, l] = charges_ref[:, l * rows:(l + 1) * rows]
    for b in range(points_ref.shape[0]):
        win[reach, leaves + b] = points_ref[b]

    peers = 1
    for off in (-4, -2, 2, 4):
        peers = peers + jnp.where((me + off >= 0) & (me + off < n), 1, 0)
    pl.semaphore_wait(barrier, peers)

    def copy(src_slot, dst_slot, sem, target):
        return pltpu.make_async_remote_copy(
            src_ref=win.at[src_slot],
            dst_ref=win.at[dst_slot],
            send_sem=send_sem.at[sem],
            recv_sem=recv_sem.at[sem],
            device_id=(target,),
            device_id_type=MESH,
        )

    direct = {off: copy(reach, reach - off, i, me + off) for i, off in enumerate((4, -4, 2, -2))}
    received = {off: copy(reach, reach + off, i, me - off) for i, off in enumerate((-4, 4, -2, 2))}
    to_sib = [(copy(reach, reach - 1, 4, sibling), core == 0), (copy(reach, reach + 1, 4, sibling), core == 1)]
    from_sib = [(copy(reach, reach + 1, 4, sibling), core == 0), (copy(reach, reach - 1, 4, sibling), core == 1)]

    def when(cond, body):
        @pl.when(cond)
        def _():
            body()

    for off in (4, -4, 2, -2):
        each(off, lambda: direct[off].start())
    for c, cond in to_sib:
        when(cond, lambda: c.start())

    forwards = [
        (4, 3, 5, 0), (-4, -3, 5, 1),
        (2, 1, 6, 0), (2, 3, 6, 1),
        (-2, -3, 7, 0), (-2, -1, 7, 1),
    ]

    def fwd(entry, act, arriving):
        held, there, sem, sender = entry
        if arriving:
            valid = (me + there >= 0) & (me + there < n) & (core == 1 - sender)
        else:
            valid = (me + held >= 0) & (me + held < n) & (core == sender)
        c = copy(reach + held, reach + there, sem, sibling)
        when(valid, lambda: act(c))

    def to_float(slot):
        for b in range(points_ref.shape[0]):
            pos[slot, b * 16:(b + 1) * 16, :] = win[slot, leaves + b].astype(f32)

    to_float(reach)
    ones = jnp.ones((1, rows), f32)

    def tail(count):
        return jnp.zeros((count, rows), f32)

    def coords(slot, l):
        return [pos[slot, pl.ds(c * leaves + l, 1), :] for c in range(3)]

    def pair(a, offset, source, vals):
        tx, ty, tz = coords(reach, a)
        sx, sy, sz = source
        shift = offset * leaf_step
        norm_t = tx * tx + ty * ty + tz * tz + (shift * shift + smoothing_sq) - (2.0 * shift) * tx
        norm_s = sx * sx + sy * sy + sz * sz
        left = jnp.concatenate([sx, sx, sy, sz, ones, ones, ones, *split3(norm_s), tail(6)], axis=0)
        right = jnp.concatenate(
            [-2.0 * tx, 2.0 * shift * ones, -2.0 * ty, -2.0 * tz, *split3(norm_t), ones, ones, ones, tail(6)], axis=0
        ).astype(bf16)
        left = left.T.astype(bf16)
        sums = []
        for t in range(rows // tile):
            total = jnp.zeros((vals.shape[0], tile), f32)
            for s in range(rows // tile):
                dist_sq = jnp.dot(
                    left[s * tile:(s + 1) * tile, :], right[:, t * tile:(t + 1) * tile], preferred_element_type=f32
                )
                block = lax.rsqrt(dist_sq.astype(bf16))
                total = total + jnp.dot(vals[:, s * tile:(s + 1) * tile], block, preferred_element_type=f32)
            sums.append(total)
        return jnp.concatenate(sums, axis=1)

    def own_leaf(a, carry):
        out_ref[a] = pair(a, 0.0, coords(reach, a), win[reach, a])
        return carry

    lax.fori_loop(0, leaves, own_leaf, 0)

    each(4, lambda: received[4].wait_recv())
    each(-4, lambda: received[-4].wait_recv())
    for entry in forwards[:2]:
        fwd(entry, lambda c: c.start(), False)
    to_float(0)
    to_float(2 * reach)

    def far_leaf(a, carry):
        ahead = near_ref[a, 1] > me * leaves + a
        source = [jnp.where(ahead, x, y) for x, y in zip(coords(2 * reach, a), coords(0, a))]
        vals = jnp.where(ahead, win[2 * reach, a], win[0, a])
        offset = jnp.where(ahead, 1.0, -1.0) * (reach * leaves)
        out_ref[a] += pair(a, offset, source, vals)
        return carry

    lax.fori_loop(0, leaves // 2, far_leaf, 0)
    each(2, lambda: received[2].wait_recv())
    each(-2, lambda: received[-2].wait_recv())
    for entry in forwards[2:]:
        fwd(entry, lambda c: c.start(), False)
    lax.fori_loop(leaves // 2, leaves, far_leaf, 0)

    for c, cond in from_sib:
        when(cond, lambda: c.wait_recv())
    for entry in forwards:
        fwd(entry, lambda c: c.wait_recv(), True)
    for slot in range(1, 2 * reach):
        if slot != reach:
            to_float(slot)

    def other(step, carry):
        a = step // (neighbours - 2)
        k = step % (neighbours - 2) + 2
        j = near_ref[a, k]
        slot = jnp.clip((j >> int(math.log2(leaves))) - me + reach, 0, 2 * reach)
        l = j & (leaves - 1)
        offset = (j - me * leaves - a).astype(f32)
        out_ref[a] += pair(a, offset, coords(slot, l), win[slot, l])
        return carry

    lax.fori_loop(0, leaves * (neighbours - 2), other, 0)

    for off in (4, -4, 2, -2):
        each(off, lambda: direct[off].wait_send())
    for c, cond in to_sib:
        when(cond, lambda: c.wait_send())
    for entry in forwards:
        fwd(entry, lambda c: c.wait_send(), False)


def dot3(a, b, transposed=False):
    dims = (((1,), (1 if transposed else 0,)), ((), ()))
    a_hi = a.astype(bf16)
    b_hi = b.astype(bf16)
    a_lo = (a - a_hi.astype(f32)).astype(bf16)
    b_lo = (b - b_hi.astype(f32)).astype(bf16)

    def one(x, y):
        return lax.dot_general(x, y, dims, preferred_element_type=f32)

    return one(a_hi, b_hi) + (one(a_lo, b_hi) + one(a_hi, b_lo))


def tree_kernel(near_scale, flags_ref, coef_ref, transfer_ref, coupling_ref, basis_ref, near_ref, out_ref, up0, up1, up2, up3):
    levels = transfer_ref.shape[0]
    group, rhs, rank = coef_ref.shape
    place = lax.axis_index("leaf") % group
    ups = (up0, up1, up2, up3)
    up0[...] = coef_ref[...]
    for t in range(levels - 1):
        count = group >> (t + 1)
        vals = ups[t][...].reshape(count, 2, rhs, rank)
        merged = dot3(vals[:, 0].reshape(count * rhs, rank), transfer_ref[t, 0]) + dot3(
            vals[:, 1].reshape(count * rhs, rank), transfer_ref[t, 1]
        )
        ups[t + 1][...] = merged.reshape(count, rhs, rank)
    coupled = []
    for t in range(levels):
        total = jnp.zeros((rhs, rank), f32)
        for m in range(1, 4):
            flag = flags_ref[0, t, m - 1].astype(f32)
            total = total + flag * dot3(ups[t][(place >> t) ^ m], coupling_ref[t, m - 1])
        coupled.append(total)
    coef = coupled[-1]
    for t in range(levels - 1, 0, -1):
        side = (place >> (t - 1)) & 1
        coef = coupled[t - 1] + dot3(coef, transfer_ref[t - 1, side], True)
    coef = coef.astype(bf16)
    leaves, rows = basis_ref.shape[:2]
    for l in range(leaves):
        far = lax.dot_general(coef, basis_ref[l], (((1,), (1,)), ((), ())), preferred_element_type=f32)
        out_ref[:, l * rows:(l + 1) * rows] = (near_ref[l] * near_scale + far).astype(bf16)


def local(n, charges, points, leaf_basis, transfer, coupling, near_list, couple_flags):
    leaves, rows, rank = leaf_basis.shape
    rhs = charges.shape[0]
    levels = transfer.shape[0]
    neighbours = near_list.shape[1]
    basis_rows = leaf_basis.reshape(leaves * rows, rank)
    first = jnp.dot(charges, basis_rows, preferred_element_type=f32)
    group = 2 ** (levels + 1)
    groups = None if n == group else [list(range(g, g + group)) for g in range(0, n, group)]
    coefs = lax.all_gather(first, "leaf", axis_index_groups=groups)
    count = 3 * leaves
    blocks = -(-count // 16)
    packed = jnp.pad(points.reshape(count, rows), ((0, blocks * 16 - count), (0, 0))).reshape(blocks, 16, rows)
    vmem = pl.BlockSpec(memory_space=pltpu.VMEM)
    smem = pl.BlockSpec(memory_space=pltpu.SMEM)
    pairs = leaves * neighbours * rows * rows
    near = pl.pallas_call(
        functools.partial(near_kernel, n, leaves, neighbours),
        out_shape=jax.ShapeDtypeStruct((leaves, rhs, rows), f32),
        in_specs=[smem, vmem, vmem],
        out_specs=vmem,
        scratch_shapes=[
            pltpu.VMEM((2 * reach + 1, leaves + blocks, 16, rows), bf16),
            pltpu.VMEM((2 * reach + 1, blocks * 16, rows), f32),
            pltpu.SemaphoreType.DMA((8,)),
            pltpu.SemaphoreType.DMA((8,)),
        ],
        compiler_params=pltpu.CompilerParams(
            collective_id=0, has_side_effects=True, vmem_limit_bytes=40 * 2**20
        ),
        cost_estimate=pl.CostEstimate(flops=pairs * 2 * 300, bytes_accessed=2**20, transcendentals=pairs),
        name="near_field",
    )(near_list, charges, packed)
    return pl.pallas_call(
        functools.partial(tree_kernel, 1.0 / math.sqrt(neighbours * rows)),
        out_shape=jax.ShapeDtypeStruct((rhs, leaves * rows), bf16),
        in_specs=[smem] + [vmem] * 5,
        out_specs=vmem,
        scratch_shapes=[pltpu.VMEM((group >> t, rhs, rank), f32) for t in range(levels)],
        compiler_params=pltpu.CompilerParams(vmem_limit_bytes=40 * 2**20),
        name="tree_far_field",
    )(couple_flags, coefs, transfer, coupling, leaf_basis, near)


def solution(mesh):
    return jax.shard_map(
        functools.partial(local, mesh.shape["leaf"]),
        mesh=mesh,
        in_specs=(
            P(None, "leaf"),
            P(None, "leaf"),
            P("leaf", None, None),
            P(),
            P(),
            P("leaf", None),
            P("leaf", None, None),
        ),
        out_specs=P(None, "leaf"),
        check_vma=False,
    )
```

time: 311 us -> 136 us (0.44)
  the two profiles are of different devices: /device:TPU:12 before, /device:TPU:5 now
where the time goes in v1:
time: 136 us
  Pallas kernels  93.8 us (69%)
  blocking collectives  39.3 us (29%)
  matrix products  2.07 us (2%)
    pallas_call x1, Pallas kernels, local(): pl.pallas_call(functools.partial(near_kernel, n, leaves, neighbours), out...  90.4 us
    all_gather x1, blocking collectives, local(): coefs = lax.all_gather(first, 'leaf', axis_index_groups=groups)  39.3 us
    pallas_call x1, Pallas kernels, local(): pl.pallas_call(functools.partial(tree_kernel, 1.0 / math.sqrt(neighbours...  3.39 us

profile of v1, /device:TPU:5, one launch (start us, length us, event | category | flops | bytes accessed | tf_op | source)
XLA Modules:
  0.0 136.3 jit_solution(10920067934211079393)
XLA Ops:
  0.0 0.0 copy-start.3
  0.0 0.0 copy-start.4
  0.0 0.0 copy-start.5
  0.0 0.8 copy.8.flags_ref
  0.8 2.1 %fusion = f32[16,128]{1,0:T(8,128)S(1)} fusion(bf16[16,8192]{1,0:T(8,128)(2,1)} %charges_ref.1, bf16[8192,128]{1,0:T(8,128)(2,1)} %bitcast.5), kind=kOutput, calls=%fused_computation | convolution fusion | flops 33554432 | bytes 2367488 | tf_op jit(solution)/shard_map/dot_general | solution.py:235
  2.9 0.0 copy-done.5
  2.9 0.1 reshape.10
  3.0 39.3 %all-gather = f32[512,128]{1,0:T(8,128)S(1)} all-gather(f32[16,128]{1,0:T(8,128)S(1)} %fusion), channel_id=2, replica_groups=mesh['leaf'=32] {'leaf'}, dimensions={0}, use_global_device_ids=true | all-gather | bytes 270336 | tf_op jit(solution)/shard_map/all_gather | solution.py:238
  42.4 0.0 copy-done.3
  42.4 0.0 copy-done.4
  42.4 0.0 copy-start
  42.4 0.0 copy-start.1
  42.4 0.0 copy-start.2
  42.4 90.4 %near_field.1.near_ref = f32[8,16,1024]{2,1,0:T(8,128)S(1)} custom-call(s32[8,5]{1,0:T(8,128)S(1)} %copy-done.4, bf16[16,8192]{1,0:T(8,128)(2,1)S(1)} %copy-done.3, bf16[2,16,1024]{2,1,0:T(8,128)(2,1)S(1)} %bitcast.7), custom_call_target="tpu_custom_call" | custom-call | flops 25165824000 | bytes 1048576 | tf_op jit(solution)/shard_map/near_field/pallas_call | solution.py:245
  132.8 0.0 copy-done
  132.8 0.0 copy-done.1
  132.9 0.0 copy-done.2
  132.9 3.4 %tree_far_field.1 = bf16[16,8192]{1,0:T(8,128)(2,1)} custom-call(s32[1,4,3]{2,1,0:T(4,128)S(1)} %copy.8.flags_ref, f32[32,16,128]{2,1,0:T(8,128)S(1)} %bitcast.6, f32[4,2,128,128]{3,2,1,0:T(8,128)S(1)} %copy-done.2, f32[4,3,128,128]{3,2,1,0:T(8,128)S(1)} %copy-done.1, bf16[8,1024,128]{2,1,0:T(8,128)(2,1)S(1)} %copy-done, f32[8,16,1024]{2,1,0:T(8,128)S(1)} %near_field.1.near_ref), custom_call_target="tpu_custom_call" | custom-call | tf_op jit(solution)/shard_map/tree_far_field/pallas_call | solution.py:262
  (1 shorter events, 0.0 us)
Async XLA Ops:
  0.0 42.4 %copy-start.3 = (bf16[16,8192]{1,0:T(8,128)(2,1)S(1)}, bf16[16,8192]{1,0:T(8,128)(2,1)}, u32[]{:S(2)}) copy-start(bf16[16,8192]{1,0:T(8,128)(2,1)} %charges_ref.1) | copy-start | bytes 786436
  0.0 42.4 %copy-start.4 = (s32[8,5]{1,0:T(8,128)S(1)}, s32[8,5]{1,0:T(8,128)}, u32[]{:S(2)}) copy-start(s32[8,5]{1,0:T(8,128)} %near_ref.1) | copy-start | bytes 484
  0.0 2.9 %copy-start.5 = (bf16[3,8192]{1,0:T(4,128)(2,1)S(1)}, bf16[3,8192]{1,0:T(4,128)(2,1)}, u32[]{:S(2)}) copy-start(bf16[3,8192]{1,0:T(4,128)(2,1)} %param.8) | copy-start | bytes 147460
  42.4 90.5 %copy-start = (bf16[8,1024,128]{2,1,0:T(8,128)(2,1)S(1)}, bf16[8,1024,128]{2,1,0:T(8,128)(2,1)}, u32[]{:S(2)}) copy-start(bf16[8,1024,128]{2,1,0:T(8,128)(2,1)} %basis_ref.1) | copy-start | bytes 6291460
  42.4 90.5 %copy-start.1 = (f32[4,3,128,128]{3,2,1,0:T(8,128)S(1)}, f32[4,3,128,128]{3,2,1,0:T(8,128)}, u32[]{:S(2)}) copy-start(f32[4,3,128,128]{3,2,1,0:T(8,128)} %coupling_ref.1) | copy-start | bytes 2359300
  42.4 90.5 %copy-start.2 = (f32[4,2,128,128]{3,2,1,0:T(8,128)S(1)}, f32[4,2,128,128]{3,2,1,0:T(8,128)}, u32[]{:S(2)}) copy-start(f32[4,2,128,128]{3,2,1,0:T(8,128)} %transfer_ref.1) | copy-start | bytes 1572868

commit v2 on v1

--- a/solution.py
+++ b/solution.py
@@ -23,7 +23,7 @@
     return hi, mid, rest - mid
 
 
-def near_kernel(n, leaves, neighbours, near_ref, charges_ref, points_ref, out_ref, win, pos, send_sem, recv_sem):
+def near_kernel(n, leaves, neighbours, near_ref, charges_ref, points_ref, first_ref, out_ref, all_ref, win, pos, coefs, send_sem, recv_sem):
     me = lax.axis_index("leaf")
     core = me % 2
     sibling = me + 1 - 2 * core
@@ -36,7 +36,10 @@
             body()
 
     barrier = pltpu.get_barrier_semaphore()
-    pl.semaphore_signal(barrier, inc=1, device_id=(sibling,), device_id_type=MESH)
+    group, rhs, rank = coefs.shape
+    steps = int(math.log2(group))
+    for partner in [sibling] + [me ^ (1 << t) for t in range(3, steps)]:
+        pl.semaphore_signal(barrier, inc=1, device_id=(partner,), device_id_type=MESH)
     for off in (-4, -2, 2, 4):
         each(off, lambda: pl.semaphore_signal(barrier, inc=1, device_id=(me + off,), device_id_type=MESH))
 
@@ -45,10 +48,32 @@
     for b in range(points_ref.shape[0]):
         win[reach, leaves + b] = points_ref[b]
 
-    peers = 1
+    peers = 1 + steps - 3
     for off in (-4, -2, 2, 4):
         peers = peers + jnp.where((me + off >= 0) & (me + off < n), 1, 0)
+    place = me % group
+    coefs[place] = first_ref[...]
     pl.semaphore_wait(barrier, peers)
+
+    def gather(t, incoming=False):
+        start = (place >> t) << t
+        if incoming:
+            start = start ^ (1 << t)
+        return pltpu.make_async_remote_copy(
+            src_ref=coefs.at[pl.ds(start, 1 << t)],
+            dst_ref=coefs.at[pl.ds(start, 1 << t)],
+            send_sem=send_sem.at[8 + t],
+            recv_sem=recv_sem.at[8 + t],
+            device_id=(me ^ (1 << t),),
+            device_id_type=MESH,
+        )
+
+    def advance(t):
+        gather(t, True).wait_recv()
+        if t + 1 < steps:
+            gather(t + 1).start()
+
+    gather(0).start()
 
     def copy(src_slot, dst_slot, sem, target):
         return pltpu.make_async_remote_copy(
@@ -109,21 +134,25 @@
         shift = offset * leaf_step
         norm_t = tx * tx + ty * ty + tz * tz + (shift * shift + smoothing_sq) - (2.0 * shift) * tx
         norm_s = sx * sx + sy * sy + sz * sz
-        left = jnp.concatenate([sx, sx, sy, sz, ones, ones, ones, *split3(norm_s), tail(6)], axis=0)
         right = jnp.concatenate(
+            [sx, sx, sy, sz, ones, ones, ones, *split3(norm_s), tail(6)], axis=0
+        ).astype(bf16)
+        left = jnp.concatenate(
             [-2.0 * tx, 2.0 * shift * ones, -2.0 * ty, -2.0 * tz, *split3(norm_t), ones, ones, ones, tail(6)], axis=0
-        ).astype(bf16)
+        )
         left = left.T.astype(bf16)
+
+        def distances(t):
+            return jnp.dot(left[t * tile:(t + 1) * tile, :], right, preferred_element_type=f32)
+
         sums = []
+        dist_sq = distances(0)
         for t in range(rows // tile):
-            total = jnp.zeros((vals.shape[0], tile), f32)
-            for s in range(rows // tile):
-                dist_sq = jnp.dot(
-                    left[s * tile:(s + 1) * tile, :], right[:, t * tile:(t + 1) * tile], preferred_element_type=f32
-                )
-                block = lax.rsqrt(dist_sq.astype(bf16))
-                total = total + jnp.dot(vals[:, s * tile:(s + 1) * tile], block, preferred_element_type=f32)
-            sums.append(total)
+            later = distances(t + 1) if t + 1 < rows // tile else None
+            block = lax.rsqrt(dist_sq.astype(bf16))
+            total = lax.dot_general(block, vals, (((1,), (1,)), ((), ())), preferred_element_type=f32)
+            sums.append(total.T)
+            dist_sq = later
         return jnp.concatenate(sums, axis=1)
 
     def own_leaf(a, carry):
@@ -131,6 +160,7 @@
         return carry
 
     lax.fori_loop(0, leaves, own_leaf, 0)
+    advance(0)
 
     each(4, lambda: received[4].wait_recv())
     each(-4, lambda: received[-4].wait_recv())
@@ -148,11 +178,13 @@
         return carry
 
     lax.fori_loop(0, leaves // 2, far_leaf, 0)
+    advance(1)
     each(2, lambda: received[2].wait_recv())
     each(-2, lambda: received[-2].wait_recv())
     for entry in forwards[2:]:
         fwd(entry, lambda c: c.start(), False)
     lax.fori_loop(leaves // 2, leaves, far_leaf, 0)
+    advance(2)
 
     for c, cond in from_sib:
         when(cond, lambda: c.wait_recv())
@@ -172,7 +204,15 @@
         out_ref[a] += pair(a, offset, coords(slot, l), win[slot, l])
         return carry
 
-    lax.fori_loop(0, leaves * (neighbours - 2), other, 0)
+    half = leaves * (neighbours - 2) // 2
+    lax.fori_loop(0, half, other, 0)
+    for t in range(3, steps - 1):
+        advance(t)
+    lax.fori_loop(half, 2 * half, other, 0)
+    advance(steps - 1)
+    all_ref[...] = coefs[...]
+    for t in range(steps):
+        gather(t).wait_send()
 
     for off in (4, -4, 2, -2):
         each(off, lambda: direct[off].wait_send())
@@ -234,31 +274,33 @@
     basis_rows = leaf_basis.reshape(leaves * rows, rank)
     first = jnp.dot(charges, basis_rows, preferred_element_type=f32)
     group = 2 ** (levels + 1)
-    groups = None if n == group else [list(range(g, g + group)) for g in range(0, n, group)]
-    coefs = lax.all_gather(first, "leaf", axis_index_groups=groups)
     count = 3 * leaves
     blocks = -(-count // 16)
     packed = jnp.pad(points.reshape(count, rows), ((0, blocks * 16 - count), (0, 0))).reshape(blocks, 16, rows)
     vmem = pl.BlockSpec(memory_space=pltpu.VMEM)
     smem = pl.BlockSpec(memory_space=pltpu.SMEM)
     pairs = leaves * neighbours * rows * rows
-    near = pl.pallas_call(
+    near, coefs = pl.pallas_call(
         functools.partial(near_kernel, n, leaves, neighbours),
-        out_shape=jax.ShapeDtypeStruct((leaves, rhs, rows), f32),
-        in_specs=[smem, vmem, vmem],
-        out_specs=vmem,
+        out_shape=(
+            jax.ShapeDtypeStruct((leaves, rhs, rows), f32),
+            jax.ShapeDtypeStruct((group, rhs, rank), f32),
+        ),
+        in_specs=[smem, vmem, vmem, vmem],
+        out_specs=(vmem, vmem),
         scratch_shapes=[
             pltpu.VMEM((2 * reach + 1, leaves + blocks, 16, rows), bf16),
             pltpu.VMEM((2 * reach + 1, blocks * 16, rows), f32),
-            pltpu.SemaphoreType.DMA((8,)),
-            pltpu.SemaphoreType.DMA((8,)),
+            pltpu.VMEM((group, rhs, rank), f32),
+            pltpu.SemaphoreType.DMA((8 + levels + 1,)),
+            pltpu.SemaphoreType.DMA((8 + levels + 1,)),
         ],
         compiler_params=pltpu.CompilerParams(
             collective_id=0, has_side_effects=True, vmem_limit_bytes=40 * 2**20
         ),
         cost_estimate=pl.CostEstimate(flops=pairs * 2 * 300, bytes_accessed=2**20, transcendentals=pairs),
         name="near_field",
-    )(near_list, charges, packed)
+    )(near_list, charges, packed, first)
     return pl.pallas_call(
         functools.partial(tree_kernel, 1.0 / math.sqrt(neighbours * rows)),
         out_shape=jax.ShapeDtypeStruct((rhs, leaves * rows), bf16),

time: 136 us -> 78.2 us (0.58)
  the two profiles are of different devices: /device:TPU:5 before, /device:TPU:9 now
where the time goes in v2:
time: 78.2 us; the launch traced here: 78 us
  Pallas kernels  74.9 us (96%)
  matrix products  2.07 us (3%)
  local copies, waits for them, and re-layouts  0.93 us (1%)
    pallas_call x1, Pallas kernels, local(): pl.pallas_call(functools.partial(near_kernel, n, leaves, neighbours), out...  71.5 us
    pallas_call x1, Pallas kernels, local(): pl.pallas_call(functools.partial(tree_kernel, 1.0 / math.sqrt(neighbours...  3.39 us
    dot_general x1, matrix products, local(): first = jnp.dot(charges, basis_rows, preferred_element_type=f32)  2.07 us

profile of v2, /device:TPU:9, one launch (start us, length us, event | category | flops | bytes accessed | tf_op | source)
XLA Modules:
  0.0 78.0 jit_solution(944525476000460209)
XLA Ops:
  0.0 0.0 copy-start.3
  0.0 0.0 copy-start.4
  0.0 0.0 copy-start.5
  0.0 0.8 %copy.8.flags_ref = s32[1,4,3]{2,1,0:T(4,128)S(1)} copy(s32[1,4,3]{1,0,2:T(1,128)} %param.13) | data formatting | bytes 96 | tf_op args[6]
  0.8 2.1 %fusion.first_ref = f32[16,128]{1,0:T(8,128)S(1)} fusion(bf16[16,8192]{1,0:T(8,128)(2,1)} %charges_ref.1, bf16[8192,128]{1,0:T(8,128)(2,1)} %bitcast.4), kind=kOutput, calls=%fused_computation | convolution fusion | flops 33554432 | bytes 2367488 | tf_op jit(solution)/shard_map/dot_general | solution.py:275
  2.9 0.0 copy-done.5
  2.9 0.1 reshape.9
  3.0 0.0 copy-done.3
  3.0 0.0 copy-done.4
  3.0 0.0 copy-start
  3.0 0.0 copy-start.1
  3.1 0.0 copy-start.2
  3.1 71.5 %near_field.1 = (f32[8,16,1024]{2,1,0:T(8,128)S(1)}, f32[32,16,128]{2,1,0:T(8,128)S(1)}) custom-call(s32[8,5]{1,0:T(8,128)S(1)} %copy-done.4, bf16[16,8192]{1,0:T(8,128)(2,1)S(1)} %copy-done.3, bf16[2,16,1024]{2,1,0:T(8,128)(2,1)S(1)} %bitcast.5, f32[16,128]{1,0:T(8,128)S(1)} %fusion.first_ref), custom_call_target="tpu_custom_call" | custom-call | flops 25165824000 | bytes 1048576 | tf_op jit(solution)/shard_map/near_field/pallas_call | solution.py:283
  74.6 0.0 copy-done
  74.6 0.0 copy-done.1
  74.6 0.0 copy-done.2
  74.6 3.4 %tree_far_field.1 = bf16[16,8192]{1,0:T(8,128)(2,1)} custom-call(s32[1,4,3]{2,1,0:T(4,128)S(1)} %copy.8.flags_ref, f32[32,16,128]{2,1,0:T(8,128)S(1)} %get-tuple-element.7.coef_ref, f32[4,2,128,128]{3,2,1,0:T(8,128)S(1)} %copy-done.2, f32[4,3,128,128]{3,2,1,0:T(8,128)S(1)} %copy-done.1, bf16[8,1024,128]{2,1,0:T(8,128)(2,1)S(1)} %copy-done, ...), custom_call_target="tpu_custom_call" | custom-call | tf_op jit(solution)/shard_map/tree_far_field/pallas_call | solution.py:304
  (1 shorter events, 0.0 us)
Async XLA Ops:
  0.0 3.0 %copy-start.3 = (bf16[16,8192]{1,0:T(8,128)(2,1)S(1)}, bf16[16,8192]{1,0:T(8,128)(2,1)}, u32[]{:S(2)}) copy-start(bf16[16,8192]{1,0:T(8,128)(2,1)} %charges_ref.1) | copy-start | bytes 786436
  0.0 3.0 %copy-start.4 = (s32[8,5]{1,0:T(8,128)S(1)}, s32[8,5]{1,0:T(8,128)}, u32[]{:S(2)}) copy-start(s32[8,5]{1,0:T(8,128)} %near_ref.1) | copy-start | bytes 484
  0.0 2.9 %copy-start.5 = (bf16[3,8192]{1,0:T(4,128)(2,1)S(1)}, bf16[3,8192]{1,0:T(4,128)(2,1)}, u32[]{:S(2)}) copy-start(bf16[3,8192]{1,0:T(4,128)(2,1)} %param.8) | copy-start | bytes 147460
  3.0 71.5 %copy-start = (bf16[8,1024,128]{2,1,0:T(8,128)(2,1)S(1)}, bf16[8,1024,128]{2,1,0:T(8,128)(2,1)}, u32[]{:S(2)}) copy-start(bf16[8,1024,128]{2,1,0:T(8,128)(2,1)} %basis_ref.1) | copy-start | bytes 6291460
  3.0 71.5 %copy-start.1 = (f32[4,3,128,128]{3,2,1,0:T(8,128)S(1)}, f32[4,3,128,128]{3,2,1,0:T(8,128)}, u32[]{:S(2)}) copy-start(f32[4,3,128,128]{3,2,1,0:T(8,128)} %coupling_ref.1) | copy-start | bytes 2359300
  3.1 71.5 %copy-start.2 = (f32[4,2,128,128]{3,2,1,0:T(8,128)S(1)}, f32[4,2,128,128]{3,2,1,0:T(8,128)}, u32[]{:S(2)}) copy-start(f32[4,2,128,128]{3,2,1,0:T(8,128)} %transfer_ref.1) | copy-start | bytes 1572868

commit v3 on v2

v3 whole, which is shorter than its diff:
```python
import functools
import math

import jax
import jax.numpy as jnp
from jax import lax
from jax.experimental import pallas as pl
from jax.experimental.pallas import tpu as pltpu
from jax.sharding import PartitionSpec as P

smoothing_sq = 0.01
reach = 4
tile = 256
f32 = jnp.float32
bf16 = jnp.bfloat16
MESH = pl.DeviceIdType.MESH


def split3(v):
    hi = v.astype(bf16).astype(f32)
    rest = v - hi
    mid = rest.astype(bf16).astype(f32)
    return hi, mid, rest - mid


def dot3(a, b, transposed=False):
    dims = (((1,), (1 if transposed else 0,)), ((), ()))
    a_hi = a.astype(bf16)
    b_hi = b.astype(bf16)
    a_lo = (a - a_hi.astype(f32)).astype(bf16)
    b_lo = (b - b_hi.astype(f32)).astype(bf16)

    def one(x, y):
        return lax.dot_general(x, y, dims, preferred_element_type=f32)

    return one(a_hi, b_hi) + (one(a_lo, b_hi) + one(a_hi, b_lo))


def kernel(
    n, leaves, neighbours, near_ref, flags_ref, charges_ref, points_ref, basis_hbm, transfer_hbm, coupling_hbm,
    out_ref, win, pos, targets, near_sum, basis, transfer, coupling, up0, up1, up2, up3, load_sem, send_sem, recv_sem,
):
    me = lax.axis_index("leaf")
    core = me % 2
    sibling = me + 1 - 2 * core
    rows = basis.shape[1]
    coefs = up0
    loads = [
        pltpu.make_async_copy(src, dst, load_sem.at[i])
        for i, (src, dst) in enumerate(((basis_hbm, basis), (transfer_hbm, transfer), (coupling_hbm, coupling)))
    ]
    for c in loads:
        c.start()
    leaf_step = 1.0 / (2.0 * reach * leaves)

    def each(off, body):
        @pl.when((me + off >= 0) & (me + off < n))
        def _():
            body()

    barrier = pltpu.get_barrier_semaphore()
    group, rhs, rank = coefs.shape
    steps = int(math.log2(group))
    for partner in [sibling] + [me ^ (1 << t) for t in range(3, steps)]:
        pl.semaphore_signal(barrier, inc=1, device_id=(partner,), device_id_type=MESH)
    for off in (-4, -2, 2, 4):
        each(off, lambda: pl.semaphore_signal(barrier, inc=1, device_id=(me + off,), device_id_type=MESH))

    for l in range(leaves):
        win[reach, l] = charges_ref[:, l * rows:(l + 1) * rows]
    for b in range(points_ref.shape[0]):
        win[reach, leaves + b] = points_ref[b]

    peers = 1 + steps - 3
    for off in (-4, -2, 2, 4):
        peers = peers + jnp.where((me + off >= 0) & (me + off < n), 1, 0)
    place = me % group
    pl.semaphore_wait(barrier, peers)

    def gather(t, incoming=False):
        start = (place >> t) << t
        if incoming:
            start = start ^ (1 << t)
        return pltpu.make_async_remote_copy(
            src_ref=coefs.at[pl.ds(start, 1 << t)],
            dst_ref=coefs.at[pl.ds(start, 1 << t)],
            send_sem=send_sem.at[8 + t],
            recv_sem=recv_sem.at[8 + t],
            device_id=(me ^ (1 << t),),
            device_id_type=MESH,
        )

    def advance(t):
        gather(t, True).wait_recv()
        if t + 1 < steps:
            gather(t + 1).start()

    def copy(src_slot, dst_slot, sem, target):
        return pltpu.make_async_remote_copy(
            src_ref=win.at[src_slot],
            dst_ref=win.at[dst_slot],
            send_sem=send_sem.at[sem],
            recv_sem=recv_sem.at[sem],
            device_id=(target,),
            device_id_type=MESH,
        )

    direct = {off: copy(reach, reach - off, i, me + off) for i, off in enumerate((4, -4, 2, -2))}
    received = {off: copy(reach, reach + off, i, me - off) for i, off in enumerate((-4, 4, -2, 2))}
    to_sib = [(copy(reach, reach - 1, 4, sibling), core == 0), (copy(reach, reach + 1, 4, sibling), core == 1)]
    from_sib = [(copy(reach, reach + 1, 4, sibling), core == 0), (copy(reach, reach - 1, 4, sibling), core == 1)]

    def when(cond, body):
        @pl.when(cond)
        def _():
            body()

    for off in (4, -4, 2, -2):
        each(off, lambda: direct[off].start())
    for c, cond in to_sib:
        when(cond, lambda: c.start())

    forwards = [
        (4, 3, 5, 0), (-4, -3, 5, 1),
        (2, 1, 6, 0), (2, 3, 6, 1),
        (-2, -3, 7, 0), (-2, -1, 7, 1),
    ]

    def fwd(entry, act, arriving):
        held, there, sem, sender = entry
        if arriving:
            valid = (me + there >= 0) & (me + there < n) & (core == 1 - sender)
        else:
            valid = (me + held >= 0) & (me + held < n) & (core == sender)
        c = copy(reach + held, reach + there, sem, sibling)
        when(valid, lambda: act(c))

    def to_float(slot):
        for b in range(points_ref.shape[0]):
            pos[slot, b * 16:(b + 1) * 16, :] = win[slot, leaves + b].astype(f32)

    loads[0].wait()
    first = jnp.zeros((rhs, rank), f32)
    for l in range(leaves):
        first = first + jnp.dot(win[reach, l], basis[l], preferred_element_type=f32)
    coefs[place] = first
    gather(0).start()

    to_float(reach)
    ones = jnp.ones((1, rows), f32)

    def tail(count):
        return jnp.zeros((count, rows), f32)

    def coords(slot, l):
        return [pos[slot, pl.ds(c * leaves + l, 1), :] for c in range(3)]

    def target(a, carry):
        tx, ty, tz = coords(reach, a)
        feats = jnp.concatenate(
            [-2.0 * tx, -2.0 * ty, -2.0 * tz, tx, *split3(tx * tx + ty * ty + tz * tz), ones, ones, ones, tail(6)],
            axis=0,
        )
        targets[a] = feats.T.astype(bf16)
        return carry

    lax.fori_loop(0, leaves, target, 0)

    def source_features(offset, source):
        sx, sy, sz = source
        shift = offset * leaf_step
        norm = sx * sx + sy * sy + sz * sz + (shift * shift + smoothing_sq) + (2.0 * shift) * sx
        return jnp.concatenate(
            [sx, sy, sz, (-2.0 * shift) * ones, ones, ones, ones, *split3(norm), tail(6)], axis=0
        ).astype(bf16)

    def near_of(a, sources):
        feats = [source_features(offset, source) for offset, source, vals in sources]
        parts = [(t, k) for t in range(rows // tile) for k in range(len(sources))]

        def distances(t, k):
            return jnp.dot(targets[a, t * tile:(t + 1) * tile, :], feats[k], preferred_element_type=f32)

        sums = []
        total = None
        dist_sq = distances(*parts[0])
        for i, (t, k) in enumerate(parts):
            later = distances(*parts[i + 1]) if i + 1 < len(parts) else None
            block = lax.rsqrt(dist_sq.astype(bf16))
            product = lax.dot_general(block, sources[k][2], (((1,), (1,)), ((), ())), preferred_element_type=f32)
            total = product if k == 0 else total + product
            if k == len(sources) - 1:
                sums.append(total.T)
            dist_sq = later
        return jnp.concatenate(sums, axis=1)

    def own_leaves(pair, carry):
        for a in (2 * pair, 2 * pair + 1):
            near_sum[a] = near_of(a, [(0.0, coords(reach, a), win[reach, a])])
        return carry

    lax.fori_loop(0, leaves // 4, own_leaves, 0)
    advance(0)
    lax.fori_loop(leaves // 4, leaves // 2, own_leaves, 0)
    advance(1)

    each(4, lambda: received[4].wait_recv())
    each(-4, lambda: received[-4].wait_recv())
    for entry in forwards[:2]:
        fwd(entry, lambda c: c.start(), False)
    to_float(0)
    to_float(2 * reach)

    def far_leaves(pair, carry):
        for a in (2 * pair, 2 * pair + 1):
            ahead = near_ref[a, 1] > me * leaves + a
            source = [jnp.where(ahead, x, y) for x, y in zip(coords(2 * reach, a), coords(0, a))]
            vals = jnp.where(ahead, win[2 * reach, a], win[0, a])
            offset = jnp.where(ahead, 1.0, -1.0) * (reach * leaves)
            near_sum[a] += near_of(a, [(offset, source, vals)])
        return carry

    lax.fori_loop(0, leaves // 4, far_leaves, 0)
    advance(2)
    each(2, lambda: received[2].wait_recv())
    each(-2, lambda: received[-2].wait_recv())
    for entry in forwards[2:]:
        fwd(entry, lambda c: c.start(), False)
    lax.fori_loop(leaves // 4, leaves // 2, far_leaves, 0)
    for t in range(3, steps):
        advance(t)

    loads[1].wait()
    loads[2].wait()
    levels = transfer.shape[0]
    ups = (up0, up1, up2, up3)
    for t in range(levels - 1):
        count = group >> (t + 1)
        vals = ups[t][...].reshape(count, 2, rhs, rank)
        merged = dot3(vals[:, 0].reshape(count * rhs, rank), transfer[t, 0]) + dot3(
            vals[:, 1].reshape(count * rhs, rank), transfer[t, 1]
        )
        ups[t + 1][...] = merged.reshape(count, rhs, rank)
    coupled = []
    for t in range(levels):
        total = jnp.zeros((rhs, rank), f32)
        for m in range(1, 4):
            flag = flags_ref[0, t, m - 1].astype(f32)
            total = total + flag * dot3(ups[t][(place >> t) ^ m], coupling[t, m - 1])
        coupled.append(total)
    coef = coupled[-1]
    for t in range(levels - 1, 0, -1):
        side = (place >> (t - 1)) & 1
        coef = coupled[t - 1] + dot3(coef, transfer[t - 1, side], True)
    coef = coef.astype(bf16)
    near_scale = 1.0 / math.sqrt(neighbours * rows)
    for l in range(leaves):
        far = lax.dot_general(coef, basis[l], (((1,), (1,)), ((), ())), preferred_element_type=f32)
        near_sum[l] = near_sum[l] * near_scale + far

    for c, cond in from_sib:
        when(cond, lambda: c.wait_recv())
    for entry in forwards:
        fwd(entry, lambda c: c.wait_recv(), True)
    for slot in range(1, 2 * reach):
        if slot != reach:
            to_float(slot)

    def others(a, carry):
        sources = []
        for k in range(2, neighbours):
            j = near_ref[a, k]
            slot = jnp.clip((j >> int(math.log2(leaves))) - me + reach, 0, 2 * reach)
            l = j & (leaves - 1)
            sources.append(((j - me * leaves - a).astype(f32), coords(slot, l), win[slot, l]))
        total = near_sum[a] + near_of(a, sources) * near_scale
        out_ref[:, pl.ds(pl.multiple_of(a * rows, rows), rows)] = total.astype(bf16)
        return carry

    lax.fori_loop(0, leaves, others, 0)

    for t in range(steps):
        gather(t).wait_send()
    for off in (4, -4, 2, -2):
        each(off, lambda: direct[off].wait_send())
    for c, cond in to_sib:
        when(cond, lambda: c.wait_send())
    for entry in forwards:
        fwd(entry, lambda c: c.wait_send(), False)


def local(n, charges, points, leaf_basis, transfer, coupling, near_list, couple_flags):
    leaves, rows, rank = leaf_basis.shape
    rhs = charges.shape[0]
    levels = transfer.shape[0]
    neighbours = near_list.shape[1]
    group = 2 ** (levels + 1)
    count = 3 * leaves
    blocks = -(-count // 16)
    packed = jnp.pad(points.reshape(count, rows), ((0, blocks * 16 - count), (0, 0))).reshape(blocks, 16, rows)
    vmem = pl.BlockSpec(memory_space=pltpu.VMEM)
    smem = pl.BlockSpec(memory_space=pltpu.SMEM)
    pairs = leaves * neighbours * rows * rows
    hbm = pl.BlockSpec(memory_space=pl.ANY)
    return pl.pallas_call(
        functools.partial(kernel, n, leaves, neighbours),
        out_shape=jax.ShapeDtypeStruct(charges.shape, bf16),
        in_specs=[smem, smem, vmem, vmem, hbm, hbm, hbm],
        out_specs=vmem,
        scratch_shapes=[
            pltpu.VMEM((2 * reach + 1, leaves + blocks, 16, rows), bf16),
            pltpu.VMEM((2 * reach + 1, blocks * 16, rows), f32),
            pltpu.VMEM((leaves, rows, 16), bf16),
            pltpu.VMEM((leaves, rhs, rows), f32),
            pltpu.VMEM(leaf_basis.shape, bf16),
            pltpu.VMEM(transfer.shape, f32),
            pltpu.VMEM(coupling.shape, f32),
            *[pltpu.VMEM((group >> t, rhs, rank), f32) for t in range(levels)],
            pltpu.SemaphoreType.DMA((3,)),
            pltpu.SemaphoreType.DMA((8 + levels + 1,)),
            pltpu.SemaphoreType.DMA((8 + levels + 1,)),
        ],
        compiler_params=pltpu.CompilerParams(
            collective_id=0, has_side_effects=True, vmem_limit_bytes=48 * 2**20
        ),
        cost_estimate=pl.CostEstimate(flops=pairs * 2 * 300, bytes_accessed=2**20, transcendentals=pairs),
        name="h2_matvec",
    )(near_list, couple_flags, charges, packed, leaf_basis, transfer, coupling)


def solution(mesh):
    return jax.shard_map(
        functools.partial(local, mesh.shape["leaf"]),
        mesh=mesh,
        in_specs=(
            P(None, "leaf"),
            P(None, "leaf"),
            P("leaf", None, None),
            P(),
            P(),
            P("leaf", None),
            P("leaf", None, None),
        ),
        out_specs=P(None, "leaf"),
        check_vma=False,
    )
```

time: 78.2 us -> 86.9 us (1.11)
  the two profiles are of different devices: /device:TPU:9 before, /device:TPU:0 now
where the time goes in v3:
time: 86.9 us; the launch traced here: 86.5 us
  Pallas kernels  78.7 us (91%)
  local copies, waits for them, and re-layouts  7.78 us (9%)
    pallas_call x1, Pallas kernels, local(): pl.pallas_call(functools.partial(kernel, n, leaves, neighbours), out_shap...  78.7 us
    unnamed x12, local copies, waits for them, and re-layouts  6.87 us

profile of v3, /device:TPU:0, one launch (start us, length us, event | category | flops | bytes accessed | tf_op | source)
XLA Modules:
  0.0 86.5 jit_solution(6431833952754251906)
XLA Ops:
  0.0 0.8 copy.8.flags_ref
  0.8 0.9 %reshape.6 = bf16[24,1024]{1,0:T(8,128)(2,1)S(1)} reshape(bf16[3,8192]{1,0:T(4,128)(2,1)} %param.8) | data formatting | bytes 98304 | tf_op jit(solution)/shard_map/reshape | solution.py:300
  1.7 0.0 copy-start
  1.7 1.6 %copy-done = bf16[8,1024,128]{2,1,0:T(8,128)(2,1)S(1)} copy-done((bf16[8,1024,128]{2,1,0:T(8,128)(2,1)S(1)}, bf16[8,1024,128]{2,1,0:T(8,128)(2,1)}, u32[]{:S(2)}) %copy-start) | copy-done | bytes 2097176
  3.3 0.0 copy-start.1
  3.3 1.1 %copy-done.1 = f32[4,3,128,128]{3,2,1,0:T(8,128)S(1)} copy-done((f32[4,3,128,128]{3,2,1,0:T(8,128)S(1)}, f32[4,3,128,128]{3,2,1,0:T(8,128)}, u32[]{:S(2)}) %copy-start.1) | copy-done | bytes 786456
  4.4 0.0 copy-start.2
  4.4 1.0 %copy-done.2 = f32[4,2,128,128]{3,2,1,0:T(8,128)S(1)} copy-done((f32[4,2,128,128]{3,2,1,0:T(8,128)S(1)}, f32[4,2,128,128]{3,2,1,0:T(8,128)}, u32[]{:S(2)}) %copy-start.2) | copy-done | bytes 524312
  5.5 0.0 copy-start.3
  5.5 0.9 %copy-done.3 = bf16[16,8192]{1,0:T(8,128)(2,1)S(1)} copy-done((bf16[16,8192]{1,0:T(8,128)(2,1)S(1)}, bf16[16,8192]{1,0:T(8,128)(2,1)}, u32[]{:S(2)}) %copy-start.3) | copy-done | bytes 262168
  6.4 0.0 copy-start.4
  6.4 0.7 copy-done.4
  7.1 78.7 %h2_matvec.1 = bf16[16,8192]{1,0:T(8,128)(2,1)S(1)} custom-call(s32[8,5]{1,0:T(8,128)S(1)} %copy-done.4, s32[1,4,3]{2,1,0:T(4,128)S(1)} %copy.8.flags_ref, bf16[16,8192]{1,0:T(8,128)(2,1)S(1)} %copy-done.3, bf16[2,16,1024]{2,1,0:T(8,128)(2,1)S(1)} %bitcast.1, bf16[8,1024,128]{2,1,0:T(8,128)(2,1)S(1)} %copy-done, f32[4,2,128,128]{3,2,1,0:T(8,128)S(1)} %copy-done.2, ...), custom_call_target="tpu_custom_call" | custom-call | flops 25165824000 | bytes 1048576 | tf_op jit(solution)/shard_map/h2_matvec/pallas_call | solution.py:305
  85.8 0.7 copy.10
  (1 shorter events, 0.0 us)
Async XLA Ops:
  1.7 1.6 %copy-start = (bf16[8,1024,128]{2,1,0:T(8,128)(2,1)S(1)}, bf16[8,1024,128]{2,1,0:T(8,128)(2,1)}, u32[]{:S(2)}) copy-start(bf16[8,1024,128]{2,1,0:T(8,128)(2,1)} %basis_hbm.1) | copy-start | bytes 6291460
  3.3 1.1 %copy-start.1 = (f32[4,3,128,128]{3,2,1,0:T(8,128)S(1)}, f32[4,3,128,128]{3,2,1,0:T(8,128)}, u32[]{:S(2)}) copy-start(f32[4,3,128,128]{3,2,1,0:T(8,128)} %coupling_hbm.1) | copy-start | bytes 2359300
  4.4 1.0 %copy-start.2 = (f32[4,2,128,128]{3,2,1,0:T(8,128)S(1)}, f32[4,2,128,128]{3,2,1,0:T(8,128)}, u32[]{:S(2)}) copy-start(f32[4,2,128,128]{3,2,1,0:T(8,128)} %transfer_hbm.1) | copy-start | bytes 1572868
  5.5 0.9 %copy-start.3 = (bf16[16,8192]{1,0:T(8,128)(2,1)S(1)}, bf16[16,8192]{1,0:T(8,128)(2,1)}, u32[]{:S(2)}) copy-start(bf16[16,8192]{1,0:T(8,128)(2,1)} %charges_ref.1) | copy-start | bytes 786436
  6.4 0.7 copy-start.4

commit v4 on v2

--- a/solution.py
+++ b/solution.py
@@ -23,7 +23,7 @@
     return hi, mid, rest - mid
 
 
-def near_kernel(n, leaves, neighbours, near_ref, charges_ref, points_ref, first_ref, out_ref, all_ref, win, pos, coefs, send_sem, recv_sem):
+def near_kernel(n, leaves, neighbours, near_ref, charges_ref, points_ref, first_ref, out_ref, all_ref, win, pos, targets, coefs, send_sem, recv_sem):
     me = lax.axis_index("leaf")
     core = me % 2
     sibling = me + 1 - 2 * core
@@ -128,35 +128,46 @@
     def coords(slot, l):
         return [pos[slot, pl.ds(c * leaves + l, 1), :] for c in range(3)]
 
-    def pair(a, offset, source, vals):
+    def target(a, carry):
         tx, ty, tz = coords(reach, a)
+        feats = jnp.concatenate(
+            [-2.0 * tx, -2.0 * ty, -2.0 * tz, tx, *split3(tx * tx + ty * ty + tz * tz), ones, ones, ones, tail(6)],
+            axis=0,
+        )
+        targets[a] = feats.T.astype(bf16)
+        return carry
+
+    lax.fori_loop(0, leaves, target, 0)
+
+    def source_features(offset, source):
         sx, sy, sz = source
         shift = offset * leaf_step
-        norm_t = tx * tx + ty * ty + tz * tz + (shift * shift + smoothing_sq) - (2.0 * shift) * tx
-        norm_s = sx * sx + sy * sy + sz * sz
-        right = jnp.concatenate(
-            [sx, sx, sy, sz, ones, ones, ones, *split3(norm_s), tail(6)], axis=0
+        norm = sx * sx + sy * sy + sz * sz + (shift * shift + smoothing_sq) + (2.0 * shift) * sx
+        return jnp.concatenate(
+            [sx, sy, sz, (-2.0 * shift) * ones, ones, ones, ones, *split3(norm), tail(6)], axis=0
         ).astype(bf16)
-        left = jnp.concatenate(
-            [-2.0 * tx, 2.0 * shift * ones, -2.0 * ty, -2.0 * tz, *split3(norm_t), ones, ones, ones, tail(6)], axis=0
-        )
-        left = left.T.astype(bf16)
-
-        def distances(t):
-            return jnp.dot(left[t * tile:(t + 1) * tile, :], right, preferred_element_type=f32)
-
-        sums = []
-        dist_sq = distances(0)
-        for t in range(rows // tile):
-            later = distances(t + 1) if t + 1 < rows // tile else None
+
+    def near_of(a, sources):
+        parts = [(s, k) for k in range(len(sources)) for s in range(rows // tile)]
+        feats = [source_features(offset, source) for offset, source, vals in sources]
+
+        def distances(s, k):
+            return jnp.dot(targets[a], feats[k][:, s * tile:(s + 1) * tile], preferred_element_type=f32)
+
+        total = None
+        dist_sq = distances(*parts[0])
+        for i, (s, k) in enumerate(parts):
+            later = distances(*parts[i + 1]) if i + 1 < len(parts) else None
             block = lax.rsqrt(dist_sq.astype(bf16))
-            total = lax.dot_general(block, vals, (((1,), (1,)), ((), ())), preferred_element_type=f32)
-            sums.append(total.T)
+            product = lax.dot_general(
+                block, sources[k][2][:, s * tile:(s + 1) * tile], (((1,), (1,)), ((), ())), preferred_element_type=f32
+            )
+            total = product if total is None else total + product
             dist_sq = later
-        return jnp.concatenate(sums, axis=1)
+        return total.T
 
     def own_leaf(a, carry):
-        out_ref[a] = pair(a, 0.0, coords(reach, a), win[reach, a])
+        out_ref[a] = near_of(a, [(0.0, coords(reach, a), win[reach, a])])
         return carry
 
     lax.fori_loop(0, leaves, own_leaf, 0)
@@ -174,7 +185,7 @@
         source = [jnp.where(ahead, x, y) for x, y in zip(coords(2 * reach, a), coords(0, a))]
         vals = jnp.where(ahead, win[2 * reach, a], win[0, a])
         offset = jnp.where(ahead, 1.0, -1.0) * (reach * leaves)
-        out_ref[a] += pair(a, offset, source, vals)
+        out_ref[a] += near_of(a, [(offset, source, vals)])
         return carry
 
     lax.fori_loop(0, leaves // 2, far_leaf, 0)
@@ -194,21 +205,20 @@
         if slot != reach:
             to_float(slot)
 
-    def other(step, carry):
-        a = step // (neighbours - 2)
-        k = step % (neighbours - 2) + 2
-        j = near_ref[a, k]
-        slot = jnp.clip((j >> int(math.log2(leaves))) - me + reach, 0, 2 * reach)
-        l = j & (leaves - 1)
-        offset = (j - me * leaves - a).astype(f32)
-        out_ref[a] += pair(a, offset, coords(slot, l), win[slot, l])
+    def others(a, carry):
+        sources = []
+        for k in range(2, neighbours):
+            j = near_ref[a, k]
+            slot = jnp.clip((j >> int(math.log2(leaves))) - me + reach, 0, 2 * reach)
+            l = j & (leaves - 1)
+            sources.append(((j - me * leaves - a).astype(f32), coords(slot, l), win[slot, l]))
+        out_ref[a] += near_of(a, sources)
         return carry
 
-    half = leaves * (neighbours - 2) // 2
-    lax.fori_loop(0, half, other, 0)
+    lax.fori_loop(0, leaves // 2, others, 0)
     for t in range(3, steps - 1):
         advance(t)
-    lax.fori_loop(half, 2 * half, other, 0)
+    lax.fori_loop(leaves // 2, leaves, others, 0)
     advance(steps - 1)
     all_ref[...] = coefs[...]
     for t in range(steps):
@@ -291,6 +301,7 @@
         scratch_shapes=[
             pltpu.VMEM((2 * reach + 1, leaves + blocks, 16, rows), bf16),
             pltpu.VMEM((2 * reach + 1, blocks * 16, rows), f32),
+            pltpu.VMEM((leaves, rows, 16), bf16),
             pltpu.VMEM((group, rhs, rank), f32),
             pltpu.SemaphoreType.DMA((8 + levels + 1,)),
             pltpu.SemaphoreType.DMA((8 + levels + 1,)),

time: 78.2 us -> 73.6 us (0.941)
  Pallas kernels: 74.9 us -> 70.3 us
    pallas_call x1, Pallas kernels: 71.5 us -> 66.9 us  [local(): pl.pallas_call(functools.partial(near_kernel, n, leaves, neighbours), out...]
where the time goes in v4:
time: 73.6 us; the launch traced here: 73.4 us
  Pallas kernels  70.3 us (96%)
  matrix products  2.07 us (3%)
  local copies, waits for them, and re-layouts  0.93 us (1%)
    pallas_call x1, Pallas kernels, local(): pl.pallas_call(functools.partial(near_kernel, n, leaves, neighbours), out...  66.9 us
    pallas_call x1, Pallas kernels, local(): pl.pallas_call(functools.partial(tree_kernel, 1.0 / math.sqrt(neighbours...  3.39 us
    dot_general x1, matrix products, local(): first = jnp.dot(charges, basis_rows, preferred_element_type=f32)  2.07 us

profile of v4, /device:TPU:9, one launch (start us, length us, event | category | flops | bytes accessed | tf_op | source)
XLA Modules:
  0.0 73.4 jit_solution(14719491119890759327)
XLA Ops:
  0.0 0.0 copy-start.3
  0.0 0.0 copy-start.4
  0.0 0.0 copy-start.5
  0.0 0.8 %copy.8.flags_ref = s32[1,4,3]{2,1,0:T(4,128)S(1)} copy(s32[1,4,3]{1,0,2:T(1,128)} %param.13) | data formatting | bytes 96 | tf_op args[6]
  0.8 2.1 %fusion.first_ref = f32[16,128]{1,0:T(8,128)S(1)} fusion(bf16[16,8192]{1,0:T(8,128)(2,1)} %charges_ref.1, bf16[8192,128]{1,0:T(8,128)(2,1)} %bitcast.4), kind=kOutput, calls=%fused_computation | convolution fusion | flops 33554432 | bytes 2367488 | tf_op jit(solution)/shard_map/dot_general | solution.py:285
  2.9 0.0 copy-done.5
  2.9 0.1 reshape.9
  3.0 0.0 copy-done.3
  3.0 0.0 copy-done.4
  3.0 0.0 copy-start
  3.0 0.0 copy-start.1
  3.1 0.0 copy-start.2
  3.1 66.9 %near_field.1 = (f32[8,16,1024]{2,1,0:T(8,128)S(1)}, f32[32,16,128]{2,1,0:T(8,128)S(1)}) custom-call(s32[8,5]{1,0:T(8,128)S(1)} %copy-done.4, bf16[16,8192]{1,0:T(8,128)(2,1)S(1)} %copy-done.3, bf16[2,16,1024]{2,1,0:T(8,128)(2,1)S(1)} %bitcast.5, f32[16,128]{1,0:T(8,128)S(1)} %fusion.first_ref), custom_call_target="tpu_custom_call" | custom-call | flops 25165824000 | bytes 1048576 | tf_op jit(solution)/shard_map/near_field/pallas_call | solution.py:293
  70.0 0.0 copy-done
  70.0 0.0 copy-done.1
  70.0 0.0 copy-done.2
  70.0 3.4 %tree_far_field.1 = bf16[16,8192]{1,0:T(8,128)(2,1)} custom-call(s32[1,4,3]{2,1,0:T(4,128)S(1)} %copy.8.flags_ref, f32[32,16,128]{2,1,0:T(8,128)S(1)} %get-tuple-element.7.coef_ref, f32[4,2,128,128]{3,2,1,0:T(8,128)S(1)} %copy-done.2, f32[4,3,128,128]{3,2,1,0:T(8,128)S(1)} %copy-done.1, bf16[8,1024,128]{2,1,0:T(8,128)(2,1)S(1)} %copy-done, ...), custom_call_target="tpu_custom_call" | custom-call | tf_op jit(solution)/shard_map/tree_far_field/pallas_call | solution.py:315
  (1 shorter events, 0.0 us)
Async XLA Ops:
  0.0 3.0 %copy-start.3 = (bf16[16,8192]{1,0:T(8,128)(2,1)S(1)}, bf16[16,8192]{1,0:T(8,128)(2,1)}, u32[]{:S(2)}) copy-start(bf16[16,8192]{1,0:T(8,128)(2,1)} %charges_ref.1) | copy-start | bytes 786436
  0.0 3.0 %copy-start.4 = (s32[8,5]{1,0:T(8,128)S(1)}, s32[8,5]{1,0:T(8,128)}, u32[]{:S(2)}) copy-start(s32[8,5]{1,0:T(8,128)} %near_ref.1) | copy-start | bytes 484
  0.0 2.9 %copy-start.5 = (bf16[3,8192]{1,0:T(4,128)(2,1)S(1)}, bf16[3,8192]{1,0:T(4,128)(2,1)}, u32[]{:S(2)}) copy-start(bf16[3,8192]{1,0:T(4,128)(2,1)} %param.8) | copy-start | bytes 147460
  3.0 66.9 %copy-start = (bf16[8,1024,128]{2,1,0:T(8,128)(2,1)S(1)}, bf16[8,1024,128]{2,1,0:T(8,128)(2,1)}, u32[]{:S(2)}) copy-start(bf16[8,1024,128]{2,1,0:T(8,128)(2,1)} %basis_ref.1) | copy-start | bytes 6291460
  3.0 66.9 %copy-start.1 = (f32[4,3,128,128]{3,2,1,0:T(8,128)S(1)}, f32[4,3,128,128]{3,2,1,0:T(8,128)}, u32[]{:S(2)}) copy-start(f32[4,3,128,128]{3,2,1,0:T(8,128)} %coupling_ref.1) | copy-start | bytes 2359300
  3.1 66.9 %copy-start.2 = (f32[4,2,128,128]{3,2,1,0:T(8,128)S(1)}, f32[4,2,128,128]{3,2,1,0:T(8,128)}, u32[]{:S(2)}) copy-start(f32[4,2,128,128]{3,2,1,0:T(8,128)} %transfer_ref.1) | copy-start | bytes 1572868

commit v5 on v4

--- a/solution.py
+++ b/solution.py
@@ -27,6 +27,8 @@
     me = lax.axis_index("leaf")
     core = me % 2
     sibling = me + 1 - 2 * core
+    side = (me // 2) % 2
+    beside = me ^ 2
     rows = out_ref.shape[-1]
     leaf_step = 1.0 / (2.0 * reach * leaves)
 
@@ -38,9 +40,9 @@
     barrier = pltpu.get_barrier_semaphore()
     group, rhs, rank = coefs.shape
     steps = int(math.log2(group))
-    for partner in [sibling] + [me ^ (1 << t) for t in range(3, steps)]:
+    for partner in [sibling, beside] + [me ^ (1 << t) for t in range(3, steps)]:
         pl.semaphore_signal(barrier, inc=1, device_id=(partner,), device_id_type=MESH)
-    for off in (-4, -2, 2, 4):
+    for off in (-4, 4):
         each(off, lambda: pl.semaphore_signal(barrier, inc=1, device_id=(me + off,), device_id_type=MESH))
 
     for l in range(leaves):
@@ -48,8 +50,8 @@
     for b in range(points_ref.shape[0]):
         win[reach, leaves + b] = points_ref[b]
 
-    peers = 1 + steps - 3
-    for off in (-4, -2, 2, 4):
+    peers = 2 + steps - 3
+    for off in (-4, 4):
         peers = peers + jnp.where((me + off >= 0) & (me + off < n), 1, 0)
     place = me % group
     coefs[place] = first_ref[...]
@@ -85,19 +87,30 @@
             device_id_type=MESH,
         )
 
-    direct = {off: copy(reach, reach - off, i, me + off) for i, off in enumerate((4, -4, 2, -2))}
-    received = {off: copy(reach, reach + off, i, me - off) for i, off in enumerate((-4, 4, -2, 2))}
+    direct = {off: copy(reach, reach - off, i, me + off) for i, off in enumerate((4, -4))}
+    received = {off: copy(reach, reach + off, i, me - off) for i, off in enumerate((-4, 4))}
     to_sib = [(copy(reach, reach - 1, 4, sibling), core == 0), (copy(reach, reach + 1, 4, sibling), core == 1)]
     from_sib = [(copy(reach, reach + 1, 4, sibling), core == 0), (copy(reach, reach - 1, 4, sibling), core == 1)]
+
+    to_beside = [(copy(reach, reach - 2, 2, beside), side == 0), (copy(reach, reach + 2, 2, beside), side == 1)]
+    from_beside = [(copy(reach, reach + 2, 2, beside), side == 0), (copy(reach, reach - 2, 2, beside), side == 1)]
+    relay_out = [
+        (copy(reach + 4, reach + 2, 3, beside), (side == 0) & (me + 4 < n)),
+        (copy(reach - 4, reach - 2, 3, beside), (side == 1) & (me - 4 >= 0)),
+    ]
+    relay_in = [
+        (copy(reach - 4, reach - 2, 3, beside), (side == 0) & (me - 2 >= 0)),
+        (copy(reach + 4, reach + 2, 3, beside), (side == 1) & (me + 2 < n)),
+    ]
 
     def when(cond, body):
         @pl.when(cond)
         def _():
             body()
 
-    for off in (4, -4, 2, -2):
+    for off in (4, -4):
         each(off, lambda: direct[off].start())
-    for c, cond in to_sib:
+    for c, cond in to_beside + to_sib:
         when(cond, lambda: c.start())
 
     forwards = [
@@ -106,12 +119,12 @@
         (-2, -3, 7, 0), (-2, -1, 7, 1),
     ]
 
-    def fwd(entry, act, arriving):
+    def fwd(entry, act, arriving, also=True):
         held, there, sem, sender = entry
         if arriving:
             valid = (me + there >= 0) & (me + there < n) & (core == 1 - sender)
         else:
-            valid = (me + held >= 0) & (me + held < n) & (core == sender)
+            valid = (me + held >= 0) & (me + held < n) & (core == sender) & also
         c = copy(reach + held, reach + there, sem, sibling)
         when(valid, lambda: act(c))
 
@@ -175,6 +188,8 @@
 
     each(4, lambda: received[4].wait_recv())
     each(-4, lambda: received[-4].wait_recv())
+    for c, cond in relay_out:
+        when(cond, lambda: c.start())
     for entry in forwards[:2]:
         fwd(entry, lambda c: c.start(), False)
     to_float(0)
@@ -190,11 +205,15 @@
 
     lax.fori_loop(0, leaves // 2, far_leaf, 0)
     advance(1)
-    each(2, lambda: received[2].wait_recv())
-    each(-2, lambda: received[-2].wait_recv())
+    for c, cond in from_beside:
+        when(cond, lambda: c.wait_recv())
     for entry in forwards[2:]:
-        fwd(entry, lambda c: c.start(), False)
+        fwd(entry, lambda c: c.start(), False, side == (0 if entry[0] > 0 else 1))
     lax.fori_loop(leaves // 2, leaves, far_leaf, 0)
+    for c, cond in relay_in:
+        when(cond, lambda: c.wait_recv())
+    for entry in forwards[2:]:
+        fwd(entry, lambda c: c.start(), False, side == (1 if entry[0] > 0 else 0))
     advance(2)
 
     for c, cond in from_sib:
@@ -224,9 +243,9 @@
     for t in range(steps):
         gather(t).wait_send()
 
-    for off in (4, -4, 2, -2):
+    for off in (4, -4):
         each(off, lambda: direct[off].wait_send())
-    for c, cond in to_sib:
+    for c, cond in to_beside + relay_out + to_sib:
         when(cond, lambda: c.wait_send())
     for entry in forwards:
         fwd(entry, lambda c: c.wait_send(), False)

time: 73.6 us -> 68.2 us (0.927)
  Pallas kernels: 70.3 us -> 64.9 us
    pallas_call x1, Pallas kernels: 66.9 us -> 61.5 us  [local(): pl.pallas_call(functools.partial(near_kernel, n, leaves, neighbours), out...]
where the time goes in v5:
time: 68.2 us; the launch traced here: 68 us
  Pallas kernels  64.9 us (95%)
  matrix products  2.07 us (3%)
  local copies, waits for them, and re-layouts  0.93 us (1%)
    pallas_call x1, Pallas kernels, local(): pl.pallas_call(functools.partial(near_kernel, n, leaves, neighbours), out...  61.5 us
    pallas_call x1, Pallas kernels, local(): pl.pallas_call(functools.partial(tree_kernel, 1.0 / math.sqrt(neighbours...  3.39 us
    dot_general x1, matrix products, local(): first = jnp.dot(charges, basis_rows, preferred_element_type=f32)  2.07 us

profile of v5, /device:TPU:9, one launch (start us, length us, event | category | flops | bytes accessed | tf_op | source)
XLA Modules:
  0.0 68.0 jit_solution(12207143738898748793)
XLA Ops:
  0.0 0.0 copy-start.3
  0.0 0.0 copy-start.4
  0.0 0.0 copy-start.5
  0.0 0.8 %copy.8.flags_ref = s32[1,4,3]{2,1,0:T(4,128)S(1)} copy(s32[1,4,3]{1,0,2:T(1,128)} %param.13) | data formatting | bytes 96 | tf_op args[6]
  0.8 2.1 %fusion.first_ref = f32[16,128]{1,0:T(8,128)S(1)} fusion(bf16[16,8192]{1,0:T(8,128)(2,1)} %charges_ref.1, bf16[8192,128]{1,0:T(8,128)(2,1)} %bitcast.4), kind=kOutput, calls=%fused_computation | convolution fusion | flops 33554432 | bytes 2367488 | tf_op jit(solution)/shard_map/dot_general | solution.py:304
  2.9 0.0 copy-done.5
  2.9 0.1 reshape.9
  3.0 0.0 copy-done.3
  3.0 0.0 copy-done.4
  3.0 0.0 copy-start
  3.0 0.0 copy-start.1
  3.1 0.0 copy-start.2
  3.1 61.5 %near_field.1 = (f32[8,16,1024]{2,1,0:T(8,128)S(1)}, f32[32,16,128]{2,1,0:T(8,128)S(1)}) custom-call(s32[8,5]{1,0:T(8,128)S(1)} %copy-done.4, bf16[16,8192]{1,0:T(8,128)(2,1)S(1)} %copy-done.3, bf16[2,16,1024]{2,1,0:T(8,128)(2,1)S(1)} %bitcast.5, f32[16,128]{1,0:T(8,128)S(1)} %fusion.first_ref), custom_call_target="tpu_custom_call" | custom-call | flops 25165824000 | bytes 1048576 | tf_op jit(solution)/shard_map/near_field/pallas_call | solution.py:312
  64.6 0.0 copy-done
  64.6 0.0 copy-done.1
  64.6 0.0 copy-done.2
  64.6 3.4 %tree_far_field.1 = bf16[16,8192]{1,0:T(8,128)(2,1)} custom-call(s32[1,4,3]{2,1,0:T(4,128)S(1)} %copy.8.flags_ref, f32[32,16,128]{2,1,0:T(8,128)S(1)} %get-tuple-element.7.coef_ref, f32[4,2,128,128]{3,2,1,0:T(8,128)S(1)} %copy-done.2, f32[4,3,128,128]{3,2,1,0:T(8,128)S(1)} %copy-done.1, bf16[8,1024,128]{2,1,0:T(8,128)(2,1)S(1)} %copy-done, ...), custom_call_target="tpu_custom_call" | custom-call | tf_op jit(solution)/shard_map/tree_far_field/pallas_call | solution.py:334
  (1 shorter events, 0.0 us)
Async XLA Ops:
  0.0 3.0 %copy-start.3 = (bf16[16,8192]{1,0:T(8,128)(2,1)S(1)}, bf16[16,8192]{1,0:T(8,128)(2,1)}, u32[]{:S(2)}) copy-start(bf16[16,8192]{1,0:T(8,128)(2,1)} %charges_ref.1) | copy-start | bytes 786436
  0.0 3.0 %copy-start.4 = (s32[8,5]{1,0:T(8,128)S(1)}, s32[8,5]{1,0:T(8,128)}, u32[]{:S(2)}) copy-start(s32[8,5]{1,0:T(8,128)} %near_ref.1) | copy-start | bytes 484
  0.0 2.9 %copy-start.5 = (bf16[3,8192]{1,0:T(4,128)(2,1)S(1)}, bf16[3,8192]{1,0:T(4,128)(2,1)}, u32[]{:S(2)}) copy-start(bf16[3,8192]{1,0:T(4,128)(2,1)} %param.8) | copy-start | bytes 147460
  3.0 61.6 %copy-start = (bf16[8,1024,128]{2,1,0:T(8,128)(2,1)S(1)}, bf16[8,1024,128]{2,1,0:T(8,128)(2,1)}, u32[]{:S(2)}) copy-start(bf16[8,1024,128]{2,1,0:T(8,128)(2,1)} %basis_ref.1) | copy-start | bytes 6291460
  3.0 61.6 %copy-start.1 = (f32[4,3,128,128]{3,2,1,0:T(8,128)S(1)}, f32[4,3,128,128]{3,2,1,0:T(8,128)}, u32[]{:S(2)}) copy-start(f32[4,3,128,128]{3,2,1,0:T(8,128)} %coupling_ref.1) | copy-start | bytes 2359300
  3.1 61.6 %copy-start.2 = (f32[4,2,128,128]{3,2,1,0:T(8,128)S(1)}, f32[4,2,128,128]{3,2,1,0:T(8,128)}, u32[]{:S(2)}) copy-start(f32[4,2,128,128]{3,2,1,0:T(8,128)} %transfer_ref.1) | copy-start | bytes 1572868

commit v6 on v5

--- a/solution.py
+++ b/solution.py
@@ -10,7 +10,7 @@
 
 smoothing_sq = 0.01
 reach = 4
-tile = 256
+tile = 512
 f32 = jnp.float32
 bf16 = jnp.bfloat16
 MESH = pl.DeviceIdType.MESH

time: 68.2 us -> 74.5 us (1.092)
  Pallas kernels: 64.9 us -> 71.2 us
    pallas_call x1, Pallas kernels: 61.5 us -> 67.9 us  [local(): pl.pallas_call(functools.partial(near_kernel, n, leaves, neighbours), out...]
where the time goes in v6:
time: 74.5 us; the launch traced here: 74.3 us
  Pallas kernels  71.2 us (96%)
  matrix products  2.07 us (3%)
  local copies, waits for them, and re-layouts  0.93 us (1%)
    pallas_call x1, Pallas kernels, local(): pl.pallas_call(functools.partial(near_kernel, n, leaves, neighbours), out...  67.9 us
    pallas_call x1, Pallas kernels, local(): pl.pallas_call(functools.partial(tree_kernel, 1.0 / math.sqrt(neighbours...  3.39 us
    dot_general x1, matrix products, local(): first = jnp.dot(charges, basis_rows, preferred_element_type=f32)  2.07 us

profile of v6, /device:TPU:9, one launch (start us, length us, event | category | flops | bytes accessed | tf_op | source)
XLA Modules:
  0.0 74.3 jit_solution(4168189321145829722)
XLA Ops:
  0.0 0.0 copy-start.3
  0.0 0.0 copy-start.4
  0.0 0.0 copy-start.5
  0.0 0.8 %copy.8.flags_ref = s32[1,4,3]{2,1,0:T(4,128)S(1)} copy(s32[1,4,3]{1,0,2:T(1,128)} %param.13) | data formatting | bytes 96 | tf_op args[6]
  0.8 2.1 %fusion.first_ref = f32[16,128]{1,0:T(8,128)S(1)} fusion(bf16[16,8192]{1,0:T(8,128)(2,1)} %charges_ref.1, bf16[8192,128]{1,0:T(8,128)(2,1)} %bitcast.4), kind=kOutput, calls=%fused_computation | convolution fusion | flops 33554432 | bytes 2367488 | tf_op jit(solution)/shard_map/dot_general | solution.py:304
  2.9 0.0 copy-done.5
  2.9 0.1 reshape.9
  3.0 0.0 copy-done.3
  3.0 0.0 copy-done.4
  3.0 0.0 copy-start
  3.0 0.0 copy-start.1
  3.1 0.0 copy-start.2
  3.1 67.9 %near_field.1 = (f32[8,16,1024]{2,1,0:T(8,128)S(1)}, f32[32,16,128]{2,1,0:T(8,128)S(1)}) custom-call(s32[8,5]{1,0:T(8,128)S(1)} %copy-done.4, bf16[16,8192]{1,0:T(8,128)(2,1)S(1)} %copy-done.3, bf16[2,16,1024]{2,1,0:T(8,128)(2,1)S(1)} %bitcast.5, f32[16,128]{1,0:T(8,128)S(1)} %fusion.first_ref), custom_call_target="tpu_custom_call" | custom-call | flops 25165824000 | bytes 1048576 | tf_op jit(solution)/shard_map/near_field/pallas_call | solution.py:312
  70.9 0.0 copy-done
  70.9 0.0 copy-done.1
  71.0 0.0 copy-done.2
  71.0 3.4 %tree_far_field.1 = bf16[16,8192]{1,0:T(8,128)(2,1)} custom-call(s32[1,4,3]{2,1,0:T(4,128)S(1)} %copy.8.flags_ref, f32[32,16,128]{2,1,0:T(8,128)S(1)} %get-tuple-element.7.coef_ref, f32[4,2,128,128]{3,2,1,0:T(8,128)S(1)} %copy-done.2, f32[4,3,128,128]{3,2,1,0:T(8,128)S(1)} %copy-done.1, bf16[8,1024,128]{2,1,0:T(8,128)(2,1)S(1)} %copy-done, ...), custom_call_target="tpu_custom_call" | custom-call | tf_op jit(solution)/shard_map/tree_far_field/pallas_call | solution.py:334
  (1 shorter events, 0.0 us)
Async XLA Ops:
  0.0 3.0 %copy-start.3 = (bf16[16,8192]{1,0:T(8,128)(2,1)S(1)}, bf16[16,8192]{1,0:T(8,128)(2,1)}, u32[]{:S(2)}) copy-start(bf16[16,8192]{1,0:T(8,128)(2,1)} %charges_ref.1) | copy-start | bytes 786436
  0.0 3.0 %copy-start.4 = (s32[8,5]{1,0:T(8,128)S(1)}, s32[8,5]{1,0:T(8,128)}, u32[]{:S(2)}) copy-start(s32[8,5]{1,0:T(8,128)} %near_ref.1) | copy-start | bytes 484
  0.0 2.9 %copy-start.5 = (bf16[3,8192]{1,0:T(4,128)(2,1)S(1)}, bf16[3,8192]{1,0:T(4,128)(2,1)}, u32[]{:S(2)}) copy-start(bf16[3,8192]{1,0:T(4,128)(2,1)} %param.8) | copy-start | bytes 147460
  3.0 67.9 %copy-start = (bf16[8,1024,128]{2,1,0:T(8,128)(2,1)S(1)}, bf16[8,1024,128]{2,1,0:T(8,128)(2,1)}, u32[]{:S(2)}) copy-start(bf16[8,1024,128]{2,1,0:T(8,128)(2,1)} %basis_ref.1) | copy-start | bytes 6291460
  3.0 67.9 %copy-start.1 = (f32[4,3,128,128]{3,2,1,0:T(8,128)S(1)}, f32[4,3,128,128]{3,2,1,0:T(8,128)}, u32[]{:S(2)}) copy-start(f32[4,3,128,128]{3,2,1,0:T(8,128)} %coupling_ref.1) | copy-start | bytes 2359300
  3.1 67.9 %copy-start.2 = (f32[4,2,128,128]{3,2,1,0:T(8,128)S(1)}, f32[4,2,128,128]{3,2,1,0:T(8,128)}, u32[]{:S(2)}) copy-start(f32[4,2,128,128]{3,2,1,0:T(8,128)} %transfer_ref.1) | copy-start | bytes 1572868
